TPU v7x, 128 devices: a whole 4x4x4 slice. The times are simulated.
128 devices in a mesh: dp: 8 (over z_hi, y), row: 4 (over z_lo, core), col: 4 (over x).
Axes of the slice: x: 4, y: 4, z: 4 (z_hi: 2, z_lo: 2; z = z_hi * 2 + z_lo), core: 2. Of those that a mesh axis runs over, the one named last changes fastest.
Arguments:
- tokens: bfloat16 [3072, 6144], P(('dp', 'row'), 'col'), may hold values from -6 to 6
- norm_scale_gain: float32 [6144], P('col'), may hold values from 0.1 to 1.9
- in_weight: bfloat16 [6144, 12288], P('col', 'row'), may hold values from -3 to 3
- out_weight: bfloat16 [12288, 6144], P('row', 'col'), may hold values from -0.0546875 to 0.0546875
- cotangent: bfloat16 [3072, 6144], P(('dp', 'row'), 'col'), may hold values from -6 to 6
Outputs:
- layer_output: bfloat16 [3072, 6144], P(('dp', 'row'), 'col')
- token_gradient: bfloat16 [3072, 6144], P(('dp', 'row'), 'col')
- gain_gradient: float32 [6144], P('col')
- grad_in_weight: bfloat16 [8, 768, 12288], P('dp', 'col', 'row')
- grad_out_weight: bfloat16 [8, 1536, 6144], P('dp', 'row', 'col')
All inputs are finite; a program needn't handle non-finite values.
Results may differ from a plain program's by a relative error of at most 0.025.
Values may be sent and summed in bfloat16 or wider, within the bound.
A program may use at most 128 MiB of HBM per device.

v0:
```python
import jax
import jax.numpy as jnp
from jax import lax
from jax.sharding import PartitionSpec as P

MODEL_WIDTH = 6144


EPS = 1e-06
CONTRACT_LAST = (((1,), (1,)), ((), ()))
CONTRACT_FIRST = (((0,), (0,)), ((), ()))


def gelu_slope(value):
    cdf = 0.5 * (1.0 + jax.scipy.special.erf(value * 0.7071067811865476))
    dens = jnp.exp(-0.5 * value * value) * 0.3989422804014327
    return cdf + value * dens


def body(tokens, norm_scale_gain, in_weight, out_weight, cotangent):
    local_float_rows = tokens.astype(jnp.float32)
    sums, squares = lax.psum(
        (jnp.sum(local_float_rows, axis=1), jnp.sum(local_float_rows * local_float_rows, axis=1)),
        "col",
    )
    local_mean = sums / MODEL_WIDTH
    local_inverse_deviation = lax.rsqrt(squares / MODEL_WIDTH - local_mean * local_mean + EPS)
    normed_own = (
        (local_float_rows - local_mean[:, None])
        * local_inverse_deviation[:, None]
        * norm_scale_gain
    ).astype(jnp.bfloat16)
    normed_full = lax.all_gather(normed_own, "row", axis=0, tiled=True)
    centered_input = (local_float_rows - local_mean[:, None]) * local_inverse_deviation[:, None]
    block = normed_full
    pre = lax.psum_scatter(
        jnp.dot(block, in_weight, preferred_element_type=jnp.float32).astype(jnp.bfloat16),
        "col",
        scatter_dimension=0,
        tiled=True,
    ).astype(jnp.float32)
    act_full = lax.all_gather(
        jax.nn.gelu(pre, approximate=False).astype(jnp.bfloat16), "col", axis=0, tiled=True
    )
    block = act_full
    branch_out = lax.psum_scatter(
        jnp.dot(block, out_weight, preferred_element_type=jnp.float32).astype(jnp.bfloat16),
        "row",
        scatter_dimension=0,
        tiled=True,
    ).astype(jnp.float32)
    layer_output = (local_float_rows + branch_out).astype(jnp.bfloat16)
    cot_full = lax.all_gather(cotangent, "row", axis=0, tiled=True)
    block = cot_full
    dact = lax.psum_scatter(
        lax.dot_general(
            block, out_weight, CONTRACT_LAST, preferred_element_type=jnp.float32
        ).astype(jnp.bfloat16),
        "col",
        scatter_dimension=0,
        tiled=True,
    ).astype(jnp.float32)
    dpre_full = lax.all_gather(
        (dact * gelu_slope(pre)).astype(jnp.bfloat16), "col", axis=0, tiled=True
    )
    block = dpre_full
    normed_cotangent = lax.psum_scatter(
        lax.dot_general(block, in_weight, CONTRACT_LAST, preferred_element_type=jnp.float32).astype(
            jnp.bfloat16
        ),
        "row",
        scatter_dimension=0,
        tiled=True,
    ).astype(jnp.float32)
    gain_gradient = lax.psum(jnp.sum(normed_cotangent * centered_input, axis=0), ("dp", "row"))
    centered_cotangent = normed_cotangent * norm_scale_gain
    leading_sum, trailing_sum = lax.psum(
        (jnp.sum(centered_cotangent, axis=1), jnp.sum(centered_cotangent * centered_input, axis=1)),
        "col",
    )
    token_gradient = (
        cotangent.astype(jnp.float32)
        + local_inverse_deviation[:, None]
        * (
            centered_cotangent
            - leading_sum[:, None] / MODEL_WIDTH
            - centered_input * trailing_sum[:, None] / MODEL_WIDTH
        )
    ).astype(jnp.bfloat16)
    columns = normed_full
    grad_in = lax.psum_scatter(
        lax.dot_general(
            columns, dpre_full, CONTRACT_FIRST, preferred_element_type=jnp.float32
        ).astype(jnp.bfloat16),
        "dp",
        scatter_dimension=0,
        tiled=True,
    )[None]
    columns = act_full
    grad_out = lax.psum_scatter(
        lax.dot_general(
            columns, cot_full, CONTRACT_FIRST, preferred_element_type=jnp.float32
        ).astype(jnp.bfloat16),
        "dp",
        scatter_dimension=0,
        tiled=True,
    )[None]
    return (layer_output, token_gradient, gain_gradient, grad_in, grad_out)


def solution(mesh):
    in_specs = (
        P(("dp", "row"), "col"),
        P("col"),
        P("col", "row"),
        P("row", "col"),
        P(("dp", "row"), "col"),
    )
    out_specs = (
        P(("dp", "row"), "col"),
        P(("dp", "row"), "col"),
        P("col"),
        P("dp", "col", "row"),
        P("dp", "row", "col"),
    )
    return jax.shard_map(body, mesh=mesh, in_specs=in_specs, out_specs=out_specs, check_vma=False)
```

profile of v0, /device:TPU:1, one launch (start us, length us, event | category | flops | bytes accessed | tf_op | source)
XLA Modules:
  0.0 525.0 jit_solution(12089288112378884749)
XLA Ops:
  7.2 0.0 all-gather.5.cloned.1.call-start
  7.2 1.1 convert_reduce_fusion
  8.4 9.3 %all-reduce.1 = (f32[96]{0:T(128)S(1)}, f32[96]{0:T(128)S(1)}) all-reduce(f32[96]{0:T(128)S(1)} %get-tuple-element.9, f32[96]{0:T(128)S(1)} %get-tuple-element.8), channel_id=1, replica_groups=mesh['dp'=8,'row'=4,'col'=4] {'col'}, use_global_device_ids=true, to_apply=%region_3.0 | all-reduce | flops 192 | bytes 1536 | tf_op jit(solution)/shard_map/psum | solution.py:22
  17.7 1.9 fusion.51
  19.6 0.0 all-gather.5.cloned.1.call-update
  19.6 0.0 all-gather.9.cloned.1.call-start
  19.6 0.7 all-gather.9.cloned.1.call-update
  20.3 0.0 reduce-scatter.7.cloned.1.call-start
  20.4 23.6 %all-gather.5.cloned.1.call-done = bf16[384,1536]{1,0:T(8,128)(2,1)} async-done(((bf16[96,1536]{1,0:T(8,128)(2,1)}), bf16[384,1536]{1,0:T(8,128)(2,1)}) %all-gather.5.cloned.1.call-update) | async-done | bytes 1179664 | tf_op jit(solution)/shard_map/all_gather | solution.py:33
  44.0 9.3 %convolution_convert_fusion.3 = bf16[384,3072]{1,0:T(8,128)(2,1)} fusion(bf16[384,1536]{1,0:T(8,128)(2,1)} %all-gather.5.cloned.1.call-done, bf16[1536,3072]{1,0:T(8,128)(2,1)} %param.7), kind=kOutput, calls=%fused_computation.3 | convolution fusion | flops 3625058304 | bytes 12976128 | tf_op jit(solution)/shard_map/dot_general | solution.py:37
  53.3 0.0 reduce-scatter.7.cloned.1.call-update
  53.3 0.0 reduce-scatter.11.cloned.1.call-start
  53.4 14.9 %all-gather.9.cloned.1.call-done = bf16[384,1536]{1,0:T(8,128)(2,1)} async-done(((bf16[96,1536]{1,0:T(8,128)(2,1)}), bf16[384,1536]{1,0:T(8,128)(2,1)}) %all-gather.9.cloned.1.call-update) | async-done | bytes 1179664 | tf_op jit(solution)/shard_map/all_gather | solution.py:53
  68.3 9.3 %convolution_convert_fusion.2 = bf16[384,3072]{1,0:T(8,128)(2,1)} fusion(bf16[384,1536]{1,0:T(8,128)(2,1)} %all-gather.9.cloned.1.call-done, bf16[3072,1536]{1,0:T(8,128)(2,1)} %param.8), kind=kOutput, calls=%fused_computation.2 | convolution fusion | flops 3625058304 | bytes 12976128 | tf_op jit(solution)/shard_map/dot_general | solution.py:56
  77.6 0.0 reduce-scatter.11.cloned.1.call-update
  77.6 0.0 all-gather.11.cloned.1.call-start
  77.7 25.4 %reduce-scatter.7.cloned.1.call-done = bf16[96,3072]{1,0:T(8,128)(2,1)} async-done(((bf16[384,3072]{1,0:T(8,128)(2,1)}), bf16[96,3072]{1,0:T(8,128)(2,1)}) %reduce-scatter.7.cloned.1.call-update) | async-done | bytes 589840 | tf_op jit(solution)/shard_map/reduce_scatter | solution.py:36
  103.1 33.8 %reduce-scatter.11.cloned.1.call-done = bf16[96,3072]{1,0:T(8,128)(2,1)} async-done(((bf16[384,3072]{1,0:T(8,128)(2,1)}), bf16[96,3072]{1,0:T(8,128)(2,1)}) %reduce-scatter.11.cloned.1.call-update) | async-done | bytes 589840 | tf_op jit(solution)/shard_map/reduce_scatter | solution.py:55
  137.0 4.9 fusion.38
  141.9 0.0 all-gather.11.cloned.1.call-update
  141.9 0.0 all-gather.7.cloned.1.call-start
  142.0 0.5 all-gather.7.cloned.1.call-update
  142.5 0.0 reduce-scatter.13.cloned.1.call-start
  142.5 32.2 %all-gather.11.cloned.1.call-done = bf16[384,3072]{1,0:T(8,128)(2,1)} async-done(((bf16[96,3072]{1,0:T(8,128)(2,1)}), bf16[384,3072]{1,0:T(8,128)(2,1)}) %all-gather.11.cloned.1.call-update) | async-done | bytes 2359312 | tf_op jit(solution)/shard_map/all_gather | solution.py:63
  174.7 9.3 %convolution_convert_fusion.4 = bf16[384,1536]{1,0:T(8,128)(2,1)} fusion(bf16[384,3072]{1,0:T(8,128)(2,1)} %all-gather.11.cloned.1.call-done, bf16[1536,3072]{1,0:T(8,128)(2,1)} %param.7), kind=kOutput, calls=%fused_computation.4 | convolution fusion | flops 3624468480 | bytes 12976128 | tf_op jit(solution)/shard_map/dot_general | solution.py:68
  184.0 0.0 reduce-scatter.13.cloned.1.call-update
  184.1 0.2 reduce-scatter.9.cloned.1.call-start
  184.3 25.6 %all-gather.7.cloned.1.call-done = bf16[384,3072]{1,0:T(8,128)(2,1)} async-done(((bf16[96,3072]{1,0:T(8,128)(2,1)}), bf16[384,3072]{1,0:T(8,128)(2,1)}) %all-gather.7.cloned.1.call-update) | async-done | bytes 2359312 | tf_op jit(solution)/shard_map/all_gather | solution.py:42
  209.9 9.4 %convolution_convert_fusion.5 = bf16[384,1536]{1,0:T(8,128)(2,1)} fusion(bf16[384,3072]{1,0:T(8,128)(2,1)} %all-gather.7.cloned.1.call-done, bf16[3072,1536]{1,0:T(8,128)(2,1)} %param.8), kind=kOutput, calls=%fused_computation.5 | convolution fusion | flops 3624468480 | bytes 12976128 | tf_op jit(solution)/shard_map/dot_general | solution.py:47
  219.3 0.0 reduce-scatter.9.cloned.1.call-update
  219.4 0.0 reduce-scatter.15.cloned.1.call-start
  219.4 1.2 copy-done.6
  220.6 7.6 %convolution_convert_fusion.1 = bf16[1536,3072]{1,0:T(8,128)(2,1)} fusion(bf16[384,1536]{1,0:T(8,128)(2,1)S(1)} %copy-done.6, bf16[384,3072]{1,0:T(8,128)(2,1)S(1)} %copy-done.4), kind=kOutput, calls=%fused_computation.1 | convolution fusion | flops 3628597248 | bytes 12976128 | tf_op jit(solution)/shard_map/dot_general | solution.py:92
  228.2 0.0 reduce-scatter.15.cloned.1.call-update
  228.3 0.0 reduce-scatter.17.cloned.1.call-start
  228.3 1.6 copy-done.3
  229.9 0.3 copy-done.5
  230.2 7.4 %convolution_convert_fusion = bf16[3072,1536]{1,0:T(8,128)(2,1)} fusion(bf16[384,3072]{1,0:T(8,128)(2,1)S(1)} %copy-done.3, bf16[384,1536]{1,0:T(8,128)(2,1)S(1)} %copy-done.5), kind=kOutput, calls=%fused_computation | convolution fusion | flops 3628597248 | bytes 12976128 | tf_op jit(solution)/shard_map/dot_general | solution.py:101
  237.7 0.0 reduce-scatter.17.cloned.1.call-update
  237.7 0.0 reduce-scatter.13.cloned.1.call-done
  237.7 0.9 copy-done
  238.6 0.0 copy-done.2
  238.6 1.4 fusion.47
  240.0 6.6 %all-reduce = (f32[96]{0:T(128)S(1)}, f32[96]{0:T(128)S(1)}) all-reduce(f32[96]{0:T(128)S(1)} %get-tuple-element.6, f32[96]{0:T(128)S(1)} %get-tuple-element.7), channel_id=1, replica_groups=mesh['dp'=8,'row'=4,'col'=4] {'col'}, use_global_device_ids=true, to_apply=%region_11.0 | all-reduce | flops 192 | bytes 1536 | tf_op jit(solution)/shard_map/psum | solution.py:77
  246.6 67.9 %psum.39 = f32[1536]{0:T(1024)} all-reduce(f32[1536]{0:T(1024)S(1)} %get-tuple-element.5), channel_id=1, replica_groups=mesh['dp'=8,'row'=4,'col'=4] {'dp','row'}, use_global_device_ids=true, to_apply=%region_13.0 | all-reduce | flops 1536 | bytes 12288 | tf_op jit(solution)/shard_map/psum | solution.py:75
  314.5 2.3 fusion.45
  316.7 73.1 %reduce-scatter.15.cloned.1.call-done = bf16[192,3072]{1,0:T(8,128)(2,1)} async-done(((bf16[1536,3072]{1,0:T(8,128)(2,1)}), bf16[192,3072]{1,0:T(8,128)(2,1)}) %reduce-scatter.15.cloned.1.call-update) | async-done | bytes 1179664 | tf_op jit(solution)/shard_map/reduce_scatter | solution.py:91
  389.8 128.4 %reduce-scatter.17.cloned.1.call-done = bf16[384,1536]{1,0:T(8,128)(2,1)} async-done(((bf16[3072,1536]{1,0:T(8,128)(2,1)}), bf16[384,1536]{1,0:T(8,128)(2,1)}) %reduce-scatter.17.cloned.1.call-update) | async-done | bytes 1179664 | tf_op jit(solution)/shard_map/reduce_scatter | solution.py:100
  (12 shorter events, 0.0 us)
Async XLA Ops:
  7.2 36.8 %all-gather.5.cloned.1.call-start = ((), (), s32[]{:S(2)}) async-start(), calls=%async_computation.6 | async-start | bytes 1474560 | tf_op jit(solution)/shard_map/all_gather | solution.py:33
  19.6 48.7 %all-gather.9.cloned.1.call-start = ((), (), s32[]{:S(2)}) async-start(), calls=%async_computation.10 | async-start | bytes 1474560 | tf_op jit(solution)/shard_map/all_gather | solution.py:53
  20.3 82.8 %reduce-scatter.7.cloned.1.call-start = ((), (), s32[]{:S(2)}) async-start(), calls=%async_computation.7 | async-start | bytes 2949120 | tf_op jit(solution)/shard_map/reduce_scatter | solution.py:36
  53.3 83.7 %reduce-scatter.11.cloned.1.call-start = ((), (), s32[]{:S(2)}) async-start(), calls=%async_computation.11 | async-start | bytes 2949120 | tf_op jit(solution)/shard_map/reduce_scatter | solution.py:55
  77.6 97.1 %all-gather.11.cloned.1.call-start = ((), (), s32[]{:S(2)}) async-start(), calls=%async_computation.12 | async-start | bytes 2949120 | tf_op jit(solution)/shard_map/all_gather | solution.py:63
  141.9 68.0 %all-gather.7.cloned.1.call-start = ((), (), s32[]{:S(2)}) async-start(), calls=%async_computation.8 | async-start | bytes 2949120 | tf_op jit(solution)/shard_map/all_gather | solution.py:42
  142.5 95.2 %reduce-scatter.13.cloned.1.call-start = ((), (), s32[]{:S(2)}) async-start(), calls=%async_computation.13 | async-start | bytes 1474560 | tf_op jit(solution)/shard_map/reduce_scatter | solution.py:67
  184.1 130.4 %reduce-scatter.9.cloned.1.call-start = ((), (), s32[]{:S(2)}) async-start(), calls=%async_computation.9 | async-start | bytes 1474560 | tf_op jit(solution)/shard_map/reduce_scatter | solution.py:46
  209.9 9.5 %copy-start.4 = (bf16[384,3072]{1,0:T(8,128)(2,1)S(1)}, bf16[384,3072]{1,0:T(8,128)(2,1)}, u32[]{:S(2)}) copy-start(bf16[384,3072]{1,0:T(8,128)(2,1)} %all-gather.11.cloned.1.call-done) | copy-start | bytes 7077892
  219.3 1.3 copy-start.6
  219.4 170.4 %reduce-scatter.15.cloned.1.call-start = ((), (), s32[]{:S(2)}) async-start(), calls=%async_computation.14 | async-start | bytes 10616832 | tf_op jit(solution)/shard_map/reduce_scatter | solution.py:91
  228.2 1.7 copy-start.3
  228.2 2.0 copy-start.5
  228.3 289.9 %reduce-scatter.17.cloned.1.call-start = ((), (), s32[]{:S(2)}) async-start(), calls=%async_computation.15 | async-start | bytes 10616832 | tf_op jit(solution)/shard_map/reduce_scatter | solution.py:100
  237.7 1.0 copy-start
  237.7 1.0 copy-start.2
  237.7 76.8 %copy-start.1 = (bf16[96,1536]{1,0:T(8,128)(2,1)S(1)}, bf16[96,1536]{1,0:T(8,128)(2,1)}, u32[]{:S(2)}) copy-start(bf16[96,1536]{1,0:T(8,128)(2,1)} %param.9) | copy-start | bytes 884740
Sparse Core Ops, SparseCore 0:
  19.7 24.2 all-gather.4
  45.7 22.5 all-gather.8
  70.7 32.3 reduce-scatter.6
  105.4 31.5 reduce-scatter.10
  142.0 32.6 all-gather.10
  176.8 33.0 all-gather.6
  212.4 21.1 reduce-scatter.12
  236.0 21.8 reduce-scatter.8
  262.4 127.3 reduce-scatter.14
  394.6 123.4 reduce-scatter.16
where the time goes:
time: 525 us
  waiting for transfers between devices  359 us (68%)
  blocking collectives  83.7 us (16%)
  matrix products  52.3 us (10%)
  between operations  14.2 us (3%)
  other arithmetic  11.6 us (2%)
    reduce_scatter x1, waiting for transfers between devices, body(): lax.psum_scatter(lax.dot_general(columns, cot_full, CONTRACT_FIRST, prefe...  128 us
    reduce_scatter x1, waiting for transfers between devices, body(): lax.psum_scatter(lax.dot_general(columns, dpre_full, CONTRACT_FIRST, pref...  73.1 us
    psum x1, blocking collectives, body(): lax.psum(jnp.sum(normed_cotangent * centered_input, axis=0), ('dp', 'row'))  67.9 us
    reduce_scatter x1, waiting for transfers between devices, body(): lax.psum_scatter(lax.dot_general(block, out_weight, CONTRACT_LAST, prefer...  33.8 us
    all_gather x1, waiting for transfers between devices, body(): lax.all_gather((dact * gelu_slope(pre)).astype(jnp.bfloat16), 'col', axis...  32.2 us
    all_gather x1, waiting for transfers between devices, body(): lax.all_gather(jax.nn.gelu(pre, approximate=False).astype(jnp.bfloat16),...  25.6 us
    reduce_scatter x1, waiting for transfers between devices, body(): lax.psum_scatter(jnp.dot(block, in_weight, preferred_element_type=jnp.flo...  25.4 us
    all_gather x1, waiting for transfers between devices, body(): normed_full = lax.all_gather(normed_own, 'row', axis=0, tiled=True)  23.6 us
  transfers between devices with their start and end apart: 10, of which 8 were waited for; matrix products, arithmetic and copies ran while one was open for 11% of the time, Pallas kernels for 0%

commit v1 on v0

v1 whole, which is shorter than its diff:
```python
import functools

import jax
import jax.numpy as jnp
from jax import lax
from jax.experimental import pallas as pl
from jax.experimental.pallas import tpu as pltpu
from jax.sharding import PartitionSpec as P

MODEL_WIDTH = 6144
EPS = 1e-06
MESH = pl.DeviceIdType.MESH
F32 = jnp.float32
BF16 = jnp.bfloat16

T = 96
G = 384
W = 1536
H = 1024
NC = 3
HALF = T // 2
FB = 192
LAST = (((1,), (1,)), ((), ()))
FIRST = (((0,), (0,)), ((), ()))


def rows(start, size, unit=16):
    return pl.ds(pl.multiple_of(start, unit), size)


def kernel(
    tok, gain, win_hbm, wout_hbm, cot,
    layer_out, token_grad, gain_grad, gin_out, gout_out,
    win, wout, nf, ngp, ngt, cg, ab, ag, dg, px, rx1, rx2, po, ro1, ro2,
    pgi, pgo, gi1, gi2, go1, go2, stat, tails, gains, wsem_in, wsem_out, osem, ssem, rsem,
):
    d, r, c = lax.axis_index("dp"), lax.axis_index("row"), lax.axis_index("col")
    zh, y = lax.div(d, 4), lax.rem(d, 4)
    zl, co = lax.div(r, 2), lax.rem(r, 2)
    cr, cl = lax.rem(c + 1, 4), lax.rem(c + 3, 4)
    yr, yl = lax.rem(y + 1, 4), lax.rem(y + 3, 4)
    cq, yq = lax.rem(c + 2, 4), lax.rem(y + 2, 4)
    XR, XL = (d, r, cr), (d, r, cl)
    YR, YL = (zh * 4 + yr, r, c), (zh * 4 + yl, r, c)
    ZL, ZH = (d, (1 - zl) * 2 + co, c), ((1 - zh) * 4 + y, r, c)
    CO = (d, zl * 2 + 1 - co, c)
    XA = (d, r, c + 1 - 2 * lax.rem(c, 2))
    XB = (d, r, 3 - c)
    YA = (zh * 4 + y + 1 - 2 * lax.rem(y, 2), r, c)
    YB = (zh * 4 + 3 - y, r, c)
    zr = (1 - zl) * 2 + co
    zc = (1 - zl) * 2 + 1 - co

    count = [0]
    sends = []

    def rc(src, dst, dev):
        i = count[0]
        count[0] += 1
        cp = pltpu.make_async_remote_copy(
            src, dst, ssem.at[i], rsem.at[i], device_id=dev, device_id_type=MESH
        )
        cp.start()
        sends.append(cp)
        return cp

    def drain(cps):
        for cp in cps:
            cp.wait_send()
        gone = [id(cp) for cp in cps]
        sends[:] = [cp for cp in sends if id(cp) not in gone]

    def win_copy(j, k):
        return pltpu.make_async_copy(
            win_hbm.at[:, rows(k * 384 + j * 128, 128, 128)],
            win.at[j, :, rows(k * 128, 128, 128)],
            wsem_in.at[j, k],
        )

    def wout_copy(j, k):
        return pltpu.make_async_copy(
            wout_hbm.at[rows(k * 384 + j * 128, 128, 128)],
            wout.at[j, rows(k * 128, 128, 128)],
            wsem_out.at[j, k],
        )

    for j in range(NC):

        @pl.loop(0, 8)
        def _(k):
            wout_copy(j, k).start()
            win_copy(j, k).start()

    def wait_wout(j):
        @pl.loop(0, 8)
        def _(k):
            wout_copy(j, k).wait()

    def wait_win(j):
        @pl.loop(0, 8)
        def _(k):
            win_copy(j, k).wait()

    barrier = pltpu.get_barrier_semaphore()
    for dev in (XR, XL, YR, YL, ZL, ZH, CO):
        pl.semaphore_signal(barrier, inc=1, device_id=dev, device_id_type=MESH)

    cg[rows(r * T, T)] = cot[...]
    x = tok[...].astype(F32)
    lane = lax.broadcasted_iota(jnp.int32, (T, 128), 1)

    def two(a, b):
        return jnp.where(lane == 0, a, jnp.where(lane == 1, b, 0.0))

    stat[0] = two(jnp.sum(x, axis=1, keepdims=True), jnp.sum(x * x, axis=1, keepdims=True))
    pl.semaphore_wait(barrier, 7)

    sa = rc(stat.at[0], stat.at[1], XA)

    def gather_row(ref, base, width=None):
        own = ref.at[rows(base + r * T, T)]
        return [rc(own, own, CO), rc(own, own, ZL)]

    def gather_row_forward(ref, base, cps):
        cps[1].wait_recv()
        blk = ref.at[rows(base + zr * T, T)]
        cps.append(rc(blk, blk, CO))

    def gather_row_end(cps):
        cps[0].wait_recv()
        cps[2].wait_recv()

    cot_g = gather_row(cg, 0)
    sa.wait_recv()
    stat[2] = stat[0] + stat[1]
    sb = rc(stat.at[2], stat.at[3], XB)
    sb.wait_recv()
    stat[4] = stat[2] + stat[3]
    mean = stat[4, :, 0:1] / MODEL_WIDTH
    inverse = lax.rsqrt(stat[4, :, 1:2] / MODEL_WIDTH - mean * mean + EPS)
    nf[rows(r * T, T)] = ((tok[...].astype(F32) - mean) * inverse * gain[...]).astype(BF16)
    nor_g = gather_row(nf, 0)
    gather_row_forward(cg, 0, cot_g)
    gather_row_end(cot_g)

    cot_h = rc(cot, cg.at[rows(G + r * T, T)], ZH)
    nor_h = rc(
        nf.at[rows(r * T, T), rows((1 - zh) * 768, 768, 128)], ngp.at[rows(r * T, T)], ZH
    )

    s1, s2 = {}, {}

    def ring_first(part, buf1, size, me_o, right, left, blk):
        h = size // 2
        return [
            rc(part.at[rows(me_o * size, h)], buf1.at[0], right),
            rc(part.at[rows(me_o * size + h, h)], buf1.at[1], left),
        ]

    def ring_second(part, buf1, buf2, size, ir, il, right, left, cps):
        h = size // 2
        cps[0].wait_recv()
        a = rows(ir * size, h)
        part[a] = (part[a].astype(F32) + buf1[0].astype(F32)).astype(BF16)
        one = rc(part.at[rows(ir * size, size)], buf2.at[0], right)
        cps[1].wait_recv()
        b = rows(il * size + h, h)
        part[b] = (part[b].astype(F32) + buf1[1].astype(F32)).astype(BF16)
        other = rc(part.at[rows(il * size, size)], buf2.at[1], left)
        return [one, other]

    def dact_part(j):
        wait_wout(j)

        @pl.loop(0, H // 256)
        def _(n):
            px[0, j % 2, :, rows(n * 256, 256, 256)] = lax.dot_general(
                cg[0:G], wout[j, rows(n * 256, 256)], LAST, preferred_element_type=F32
            ).astype(BF16)

        s1[0, j] = ring_first(px.at[0, j % 2], rx1.at[0, j], T, cq, XR, XL, None)

    def pre_part(j):
        wait_win(j)

        @pl.loop(0, H // 256)
        def _(n):
            px[1, j % 2, :, rows(n * 256, 256, 256)] = jnp.dot(
                nf[...], win[j, :, rows(n * 256, 256, 256)], preferred_element_type=F32
            ).astype(BF16)

        s1[1, j] = ring_first(px.at[1, j % 2], rx1.at[1, j], T, cq, XR, XL, None)

    def rs_second(kind, j):
        s2[kind, j] = ring_second(
            px.at[kind, j % 2], rx1.at[kind, j], rx2.at[kind, j], T, cr, cl, XR, XL, s1[kind, j]
        )

    gat = {}

    def gather_x(key, ref, base):
        own = ref.at[rows(base + c * T, T)]
        gat[key] = [rc(own, own, XR), rc(own, own, XL)]

    def gather_x_forward(key, ref, base):
        cps = gat[key]
        cps[0].wait_recv()
        a = ref.at[rows(base + cl * T, HALF)]
        cps.append(rc(a, a, XR))
        cps[1].wait_recv()
        b = ref.at[rows(base + cr * T + HALF, HALF)]
        cps.append(rc(b, b, XL))

    def gather_x_end(key):
        gat[key][2].wait_recv()
        gat[key][3].wait_recv()

    zsend = {}

    def activate(j):
        for kind in (0, 1):
            for cp in s2[kind, j]:
                cp.wait_recv()

        @pl.loop(0, H // 256)
        def _(n):
            at = rows(n * 256, 256, 256)
            own = rows(c * T, T)
            dact = (
                px[0, j % 2, own, at].astype(F32)
                + rx2[0, j, 0, :, at].astype(F32)
                + rx2[0, j, 1, :, at].astype(F32)
            )
            pre = (
                px[1, j % 2, own, at].astype(F32)
                + rx2[1, j, 0, :, at].astype(F32)
                + rx2[1, j, 1, :, at].astype(F32)
            )
            cdf = 0.5 * (1.0 + lax.erf(pre * 0.7071067811865476))
            dens = jnp.exp(-0.5 * pre * pre) * 0.3989422804014327
            ab[j, own, at] = (pre * cdf).astype(BF16)
            dg[j, own, at] = (dact * (cdf + pre * dens)).astype(BF16)

        gather_x(("a", j), ab.at[j], 0)
        gather_x(("d", j), dg.at[j], 0)
        zsend["a", j] = rc(
            ab.at[j, rows(c * T, T), rows((1 - zh) * 512, 512, 128)],
            ag.at[j, rows(G + c * T, T)],
            ZH,
        )
        zsend["d", j] = rc(dg.at[j, rows(c * T, T)], dg.at[j, rows(G + c * T, T)], ZH)

    def gather_forward(j):
        gather_x_forward(("a", j), ab.at[j], 0)
        gather_x_forward(("d", j), dg.at[j], 0)
        zsend["a", j].wait_recv()
        gather_x(("ap", j), ag.at[j], G)
        zsend["d", j].wait_recv()
        gather_x(("dp", j), dg.at[j], G)

    def partner_forward(j):
        gather_x_forward(("ap", j), ag.at[j], G)
        gather_x_forward(("dp", j), dg.at[j], G)

    y1, y2 = {}, {}

    def grad_out_part(j):
        gather_x_end(("a", j))
        ag[j, 0:G] = ab[j, :, rows(zh * 512, 512, 128)]
        gather_x_end(("ap", j))
        if j >= 2:
            drain(y1["o", j - 2] + y2["o", j - 2])
        part = pgo.at[j % 2]

        def block(b):
            at = rows(b * 128, 128, 128)
            part[at] = lax.dot_general(
                ag[j, :, at], cg[...], FIRST, preferred_element_type=F32
            ).astype(BF16)

        block(yq)
        y1["o", j] = ring_first(part, go1.at[j], 128, yq, YR, YL, None)

        @pl.loop(1, 4)
        def _(i):
            block(lax.rem(yq + i, 4))

    def grad_in_part(j):
        gather_x_end(("d", j))
        gather_x_end(("dp", j))
        if j >= 2:
            drain(y1["i", j - 2] + y2["i", j - 2])
        part = pgi.at[j % 2]

        def block(b):
            at = rows(b * FB, FB)
            part[at] = jnp.dot(ngt[at], dg[j], preferred_element_type=F32).astype(BF16)

        block(yq)
        y1["i", j] = ring_first(part, gi1.at[j], FB, yq, YR, YL, None)

        @pl.loop(1, 4)
        def _(i):
            block(lax.rem(yq + i, 4))

    def grad_second(key, j):
        if key == "o":
            y2["o", j] = ring_second(
                pgo.at[j % 2], go1.at[j], go2.at[j], 128, yr, yl, YR, YL, y1["o", j]
            )
        else:
            y2["i", j] = ring_second(
                pgi.at[j % 2], gi1.at[j], gi2.at[j], FB, yr, yl, YR, YL, y1["i", j]
            )

    ocps = []

    def grad_end(key, j):
        for cp in y2[key, j]:
            cp.wait_recv()
        part, buf, size, out = (
            (pgo, go2, 128, gout_out) if key == "o" else (pgi, gi2, FB, gin_out)
        )
        own = rows(y * size, size)
        buf[j, 0] = (
            part[j % 2, own].astype(F32) + buf[j, 0].astype(F32) + buf[j, 1].astype(F32)
        ).astype(BF16)
        cp = pltpu.make_async_copy(
            buf.at[j, 0], out.at[j], osem.at[0 if key == "o" else 1, j]
        )
        cp.start()
        ocps.append(cp)

    dact_part(0)
    gather_row_forward(nf, 0, nor_g)
    gather_row_end(nor_g)
    pre_part(0)
    rs_second(0, 0)
    rs_second(1, 0)
    dact_part(1)
    pre_part(1)
    activate(0)
    cot_h.wait_recv()
    cot_pg = gather_row(cg, G)
    nor_h.wait_recv()
    nor_pg = gather_row(ngp, 0)
    rs_second(0, 1)
    rs_second(1, 1)
    gather_forward(0)
    drain(s1[0, 0] + s2[0, 0])
    dact_part(2)
    drain(s1[1, 0] + s2[1, 0])
    pre_part(2)
    ngt[:, 0:G] = jnp.transpose(nf[:, rows(zh * 768, 768, 128)])
    gather_row_forward(cg, G, cot_pg)
    gather_row_forward(ngp, 0, nor_pg)
    activate(1)
    gather_row_end(cot_pg)
    gather_row_end(nor_pg)
    ngt[:, G:] = jnp.transpose(ngp[...])
    partner_forward(0)
    rs_second(0, 2)
    rs_second(1, 2)
    gather_forward(1)
    grad_out_part(0)
    activate(2)
    grad_in_part(0)
    partner_forward(1)
    gather_forward(2)
    grad_second("o", 0)
    grad_second("i", 0)
    grad_out_part(1)
    grad_in_part(1)
    partner_forward(2)
    grad_end("o", 0)
    grad_second("o", 1)
    grad_end("i", 0)
    grad_second("i", 1)
    grad_out_part(2)
    grad_in_part(2)

    def row_first(q):
        return [
            rc(po.at[q, rows((z * 2 + 1 - co) * T, T)], ro1.at[q, z], CO) for z in (0, 1)
        ]

    def row_second(q, cps):
        for z in (0, 1):
            cps[z].wait_recv()
            at = rows((z * 2 + co) * T, T)
            po[q, at] = (po[q, at].astype(F32) + ro1[q, z].astype(F32)).astype(BF16)
        return rc(po.at[q, rows(zr * T, T)], ro2.at[q], ZL)

    @pl.loop(0, W // 256)
    def _(n):
        at = rows(n * 256, 256, 256)
        total = lax.dot_general(dg[0, 0:G], win[0, at], LAST, preferred_element_type=F32)
        for j in range(1, NC):
            total += lax.dot_general(dg[j, 0:G], win[j, at], LAST, preferred_element_type=F32)
        po[1, :, at] = total.astype(BF16)

    dn1 = row_first(1)

    @pl.loop(0, W // 256)
    def _(n):
        at = rows(n * 256, 256, 256)
        total = jnp.dot(ab[0], wout[0, :, at], preferred_element_type=F32)
        for j in range(1, NC):
            total += jnp.dot(ab[j], wout[j, :, at], preferred_element_type=F32)
        po[0, :, at] = total.astype(BF16)

    lo1 = row_first(0)
    dn2 = row_second(1, dn1)
    lo2 = row_second(0, lo1)
    grad_end("o", 1)
    grad_second("o", 2)
    grad_end("i", 1)
    grad_second("i", 2)

    dn2.wait_recv()
    own = rows(r * T, T)
    mean = stat[4, :, 0:1] / MODEL_WIDTH
    inverse = lax.rsqrt(stat[4, :, 1:2] / MODEL_WIDTH - mean * mean + EPS)
    dnorm = po[1, own].astype(F32) + ro2[1].astype(F32)
    xhat = (tok[...].astype(F32) - mean) * inverse
    gains[0] = jnp.sum((dnorm * xhat).reshape(T // 8, 8, W), axis=0)
    ga = rc(gains.at[0], gains.at[1], CO)
    dxhat = dnorm * gain[...]
    tails[0] = two(
        jnp.sum(dxhat, axis=1, keepdims=True), jnp.sum(dxhat * xhat, axis=1, keepdims=True)
    )
    ta = rc(tails.at[0], tails.at[1], XA)
    ta.wait_recv()
    tails[2] = tails[0] + tails[1]
    tb = rc(tails.at[2], tails.at[3], XB)
    ga.wait_recv()
    gains[2] = gains[0] + gains[1]
    gb = rc(gains.at[2], gains.at[3], ZL)
    tb.wait_recv()
    tails[4] = tails[2] + tails[3]
    first = tails[4, :, 0:1] / MODEL_WIDTH
    second = tails[4, :, 1:2] / MODEL_WIDTH
    dnorm = po[1, own].astype(F32) + ro2[1].astype(F32)
    xhat = (tok[...].astype(F32) - mean) * inverse
    token_grad[...] = (
        cot[...].astype(F32) + inverse * (dnorm * gain[...] - first - xhat * second)
    ).astype(BF16)
    gb.wait_recv()
    gains[4] = gains[2] + gains[3]
    gc = rc(gains.at[4], gains.at[5], ZH)
    lo2.wait_recv()
    layer_out[...] = (
        tok[...].astype(F32) + (po[0, own].astype(F32) + ro2[0].astype(F32))
    ).astype(BF16)
    gc.wait_recv()
    gains[6] = gains[4] + gains[5]
    gd = rc(gains.at[6], gains.at[7], YA)
    gd.wait_recv()
    gains[8] = gains[6] + gains[7]
    ge = rc(gains.at[8], gains.at[9], YB)
    ge.wait_recv()
    gain_grad[...] = jnp.sum(gains[8] + gains[9], axis=0, keepdims=True)
    grad_end("o", 2)
    grad_end("i", 2)
    drain(list(sends))
    for cp in ocps:
        cp.wait()
    assert count[0] == N_COPIES, count[0]


N_COPIES = 131


def body(tokens, norm_scale_gain, in_weight, out_weight, cotangent):
    vm = pl.BlockSpec(memory_space=pltpu.VMEM)
    hbm = pl.BlockSpec(memory_space=pl.ANY)
    layer_out, token_grad, gain_grad, gin, gout = pl.pallas_call(
        kernel,
        out_shape=(
            jax.ShapeDtypeStruct((T, W), BF16),
            jax.ShapeDtypeStruct((T, W), BF16),
            jax.ShapeDtypeStruct((1, W), F32),
            jax.ShapeDtypeStruct((NC, FB, H), BF16),
            jax.ShapeDtypeStruct((NC, 128, W), BF16),
        ),
        in_specs=[vm, vm, hbm, hbm, vm],
        out_specs=(vm, vm, vm, hbm, hbm),
        scratch_shapes=[
            pltpu.VMEM((NC, W, H), BF16),
            pltpu.VMEM((NC, H, W), BF16),
            pltpu.VMEM((G, W), BF16),
            pltpu.VMEM((G, 768), BF16),
            pltpu.VMEM((768, 2 * G), BF16),
            pltpu.VMEM((2 * G, W), BF16),
            pltpu.VMEM((NC, G, H), BF16),
            pltpu.VMEM((NC, 2 * G, 512), BF16),
            pltpu.VMEM((NC, 2 * G, H), BF16),
            pltpu.VMEM((2, 2, G, H), BF16),
            pltpu.VMEM((2, NC, 2, HALF, H), BF16),
            pltpu.VMEM((2, NC, 2, T, H), BF16),
            pltpu.VMEM((2, G, W), BF16),
            pltpu.VMEM((2, 2, T, W), BF16),
            pltpu.VMEM((2, T, W), BF16),
            pltpu.VMEM((2, 768, H), BF16),
            pltpu.VMEM((2, 512, W), BF16),
            pltpu.VMEM((NC, 2, FB // 2, H), BF16),
            pltpu.VMEM((NC, 2, FB, H), BF16),
            pltpu.VMEM((NC, 2, 64, W), BF16),
            pltpu.VMEM((NC, 2, 128, W), BF16),
            pltpu.VMEM((5, T, 128), F32),
            pltpu.VMEM((5, T, 128), F32),
            pltpu.VMEM((10, 8, W), F32),
            pltpu.SemaphoreType.DMA((NC, 8)),
            pltpu.SemaphoreType.DMA((NC, 8)),
            pltpu.SemaphoreType.DMA((2, NC)),
            pltpu.SemaphoreType.DMA((N_COPIES,)),
            pltpu.SemaphoreType.DMA((N_COPIES,)),
        ],
        compiler_params=pltpu.CompilerParams(
            collective_id=0, has_side_effects=True, vmem_limit_bytes=62 * 2**20
        ),
        cost_estimate=pl.CostEstimate(
            flops=22 * 10**9, bytes_accessed=24 * 10**6, transcendentals=600000
        ),
        name="feed_forward",
    )(tokens, norm_scale_gain.reshape(1, W), in_weight, out_weight, cotangent)
    grad_in = gin.reshape(NC, FB, 8, 128).transpose(1, 2, 0, 3).reshape(1, FB, NC * H)
    grad_out = gout.reshape(1, NC * 128, W)
    return (layer_out, token_grad, gain_grad.reshape(W), grad_in, grad_out)


def solution(mesh):
    in_specs = (
        P(("dp", "row"), "col"),
        P("col"),
        P("col", "row"),
        P("row", "col"),
        P(("dp", "row"), "col"),
    )
    out_specs = (
        P(("dp", "row"), "col"),
        P(("dp", "row"), "col"),
        P("col"),
        P("dp", "col", "row"),
        P("dp", "row", "col"),
    )
    return jax.shard_map(body, mesh=mesh, in_specs=in_specs, out_specs=out_specs, check_vma=False)
```

time: 525 us -> 203 us (0.39)
  waiting for transfers between devices: 359 us -> 0 us
  Pallas kernels: 0 us -> 192 us
  blocking collectives: 83.7 us -> 0 us
  matrix products: 52.3 us -> 0 us
  between operations: 14.2 us -> 0.68 us
  other arithmetic: 11.6 us -> 0.62 us
    reduce_scatter x6 -> x0, waiting for transfers between devices: 261 us -> none  [the longest x1 128 us: body(): lax.psum_scatter(lax.dot_general(columns, cot_full, CONTRACT_FIRST, prefe...]
    pallas_call x0 -> x1, Pallas kernels: none -> 192 us  [body(): pl.pallas_call(kernel, out_shape=(jax.ShapeDtypeStruct((T, W), BF16), jax...]
    all_gather x4 -> x0, waiting for transfers between devices: 96.4 us -> none  [the longest x1 32.2 us: body(): lax.all_gather((dact * gelu_slope(pre)).astype(jnp.bfloat16), 'col', axis...]
    psum x3 -> x0, blocking collectives: 83.7 us -> none  [the longest x1 67.9 us: body(): lax.psum(jnp.sum(normed_cotangent * centered_input, axis=0), ('dp', 'row'))]
    dot_general x6 -> x0, matrix products: 52.3 us -> none  [the longest x1 9.39 us: body(): jnp.dot(block, out_weight, preferred_element_type=jnp.float32)]
    convert_element_type x3 -> x0, other arithmetic: 9.06 us -> none  [the longest x1 4.91 us: body(): (dact * gelu_slope(pre)).astype(jnp.bfloat16)]
  transfers between devices with their start and end apart: 10 -> 0, of which waited for: 8 -> 0; matrix products, arithmetic and copies ran while one was open for 11% -> 0% of each run, Pallas kernels for 0% -> 0%
where the time goes in v1:
time: 203 us; the launch traced here: 202 us
  Pallas kernels  192 us (95%)
  local copies, waits for them, and re-layouts  9.17 us (5%)
    pallas_call x1, Pallas kernels, body(): pl.pallas_call(kernel, out_shape=(jax.ShapeDtypeStruct((T, W), BF16), jax...  192 us

profile of v1, /device:TPU:1, one launch (start us, length us, event | category | flops | bytes accessed | tf_op | source)
XLA Modules:
  0.0 202.4 jit_solution(4639710714330206449)
XLA Ops:
  0.6 1.3 reshape.25.gain
  1.9 191.9 %feed_forward.1 = (bf16[96,1536]{1,0:T(8,128)(2,1)}, bf16[96,1536]{1,0:T(8,128)(2,1)}, f32[1,1536]{1,0:T(1,128)}, bf16[3,192,1024]{2,1,0:T(8,128)(2,1)}, bf16[3,128,1536]{2,1,0:T(8,128)(2,1)}) custom-call(bf16[96,1536]{1,0:T(8,128)(2,1)} %tok.1, f32[1,1536]{1,0:T(1,128)} %reshape.25.gain, bf16[1536,3072]{1,0:T(8,128)(2,1)} %win_hbm.1, ...), custom_call_target="tpu_custom_call" | custom-call | flops 22000001024 | bytes 24000000 | tf_op jit(solution)/shard_map/feed_forward/pallas_call | solution.py:477
  193.9 1.6 copy.12
  195.4 1.6 copy.14
  197.1 0.0 copy-start.3
  197.1 0.0 copy-start.2
  197.1 0.0 copy-start.1
  197.1 2.2 %reshape.28 = bf16[1,192,3072]{2,1,0:T(8,128)(2,1)} reshape(bf16[192,8,3,128]{3,2,1,0:T(4,128)(2,1)S(1)} %bitcast.8) | data formatting | bytes 2359296 | tf_op jit(solution)/shard_map/reshape | solution.py:527
  199.3 0.0 copy-start
  199.3 0.0 copy-done.3
  199.3 0.6 reduce
  199.9 0.0 copy-done.2
  199.9 0.7 copy.18
  200.7 0.0 copy-done.1
  200.7 0.7 copy.19
  201.4 0.0 copy-done
  201.4 1.0 copy.20
Async XLA Ops:
  197.1 2.2 %copy-start.3 = (f32[1,1536]{1,0:T(1,128)S(1)}, f32[1,1536]{1,0:T(1,128)}, u32[]{:S(2)}) copy-start(f32[1,1536]{1,0:T(1,128)} %get-tuple-element.12) | copy-start | bytes 18436
  197.1 2.9 %copy-start.2 = (bf16[96,1536]{1,0:T(8,128)(2,1)S(1)}, bf16[96,1536]{1,0:T(8,128)(2,1)}, u32[]{:S(2)}) copy-start(bf16[96,1536]{1,0:T(8,128)(2,1)} %get-tuple-element.20) | copy-start | bytes 884740
  197.1 3.6 %copy-start.1 = (bf16[96,1536]{1,0:T(8,128)(2,1)S(1)}, bf16[96,1536]{1,0:T(8,128)(2,1)}, u32[]{:S(2)}) copy-start(bf16[96,1536]{1,0:T(8,128)(2,1)} %get-tuple-element.21) | copy-start | bytes 884740
  199.3 2.1 %copy-start = (bf16[3,128,1536]{2,1,0:T(8,128)(2,1)S(1)}, bf16[3,128,1536]{2,1,0:T(8,128)(2,1)}, u32[]{:S(2)}) copy-start(bf16[3,128,1536]{2,1,0:T(8,128)(2,1)} %get-tuple-element.14) | copy-start | bytes 3538948

commit v2 on v0

v2 whole, which is shorter than its diff:
```python
import jax
import jax.numpy as jnp
from jax import lax
from jax.experimental import pallas as pl
from jax.experimental.pallas import tpu as pltpu
from jax.sharding import PartitionSpec as P

MODEL_WIDTH = 6144
EPS = 1e-06
MESH = pl.DeviceIdType.MESH
F32 = jnp.float32
BF16 = jnp.bfloat16

T = 96
G = 384
W = 1536
H = 1024
NC = 3
HALF = T // 2
FB = 192
FG = 4 * FB
LAST = (((1,), (1,)), ((), ()))
FIRST = (((0,), (0,)), ((), ()))

ACT_WAY = (2, 2, 2)
DPRE_WAY = (2, 2, 2)
SPLIT_DACT = (0, 1)
SPLIT_PRE = (0,)
SPLIT_IN = (2,)
SPLIT_OUT = ()

ORDER = (
    "cotg", "st1", "dact1a", "st2", "dact0a", "rsd1a", "st3", "coth", "rsd0a", "cotf", "dact1b",
    "dact0b", "pre0a", "rsd1b", "norf", "rsd0b", "pre0b", "rsp0a", "pre1", "cph", "rsp0b", "rsp1",
    "norh", "act0", "dact2", "af0", "cpf", "sd0", "za0", "nph", "ap0", "act1", "npf", "zaq0",
    "ngt0", "df0", "zd0", "sd1", "go0", "pre2", "zdq0", "dp0", "ngt1", "gso0", "af1", "zd1", "df1",
    "rsp2", "rsd2", "gi0", "za1", "ap1", "dp1", "gsi0", "zaq1", "zdq1", "act2", "go1", "za2",
    "zd2", "gi1", "sd2", "gso1", "dna", "gsi1", "af2", "geo0", "df2", "zaq2", "ap2", "dnb", "go2",
    "dp2", "zdq2", "dn2", "out", "gei0", "gei1", "gi2", "gso2", "gsi2a", "fin", "gb", "gc", "lo2",
    "gd", "geo1", "gsi2b", "t2", "geo2", "lo3", "gei2a", "ge", "t3", "gei2b", "gz",
)


def rows(start, size, unit=16):
    return pl.ds(pl.multiple_of(start, unit), size)


def kernel(
    tok, gain, win_hbm, wout_hbm, cot,
    layer_out, token_grad, gain_grad, gin_out, gout_out,
    win, wout, nf, ngp, ngt, cg, ab, ag, dg, px, rx1, rx2, po, ro1, ro2, acc,
    pgi, pgo, gi1, gi2, go1, go2, stat, tails, gains, wsem_in, wsem_out, osem, ssem, rsem,
):
    d, r, c = lax.axis_index("dp"), lax.axis_index("row"), lax.axis_index("col")
    zh, y = lax.div(d, 4), lax.rem(d, 4)
    zl, co = lax.div(r, 2), lax.rem(r, 2)
    cr, cl = lax.rem(c + 1, 4), lax.rem(c + 3, 4)
    yr, yl = lax.rem(y + 1, 4), lax.rem(y + 3, 4)
    cq, yq = lax.rem(c + 2, 4), lax.rem(y + 2, 4)
    XR, XL = (d, r, cr), (d, r, cl)
    YR, YL = (zh * 4 + yr, r, c), (zh * 4 + yl, r, c)
    ZL, ZH = (d, (1 - zl) * 2 + co, c), ((1 - zh) * 4 + y, r, c)
    CO = (d, zl * 2 + 1 - co, c)
    XA = (d, r, c + 1 - 2 * lax.rem(c, 2))
    XB = (d, r, 3 - c)
    YA = (zh * 4 + y + 1 - 2 * lax.rem(y, 2), r, c)
    YB = (zh * 4 + 3 - y, r, c)

    def slot(ref, i, first=0):
        return ref.at[pl.ds(first + 2 * (i % 2), 2), i // 2]

    count = [0]
    sends = []
    V = {}

    def rc(src, dst, dev):
        i = count[0]
        count[0] += 1
        cp = pltpu.make_async_remote_copy(
            src, dst, ssem.at[i], rsem.at[i], device_id=dev, device_id_type=MESH
        )
        cp.start()
        sends.append(cp)
        return cp

    def recv(*cps):
        for cp in cps:
            cp.wait_recv()

    def drain(cps):
        for cp in cps:
            cp.wait_send()
        gone = [id(cp) for cp in cps]
        sends[:] = [cp for cp in sends if id(cp) not in gone]

    def win_copy(j, k):
        return pltpu.make_async_copy(
            win_hbm.at[:, rows(k * 384 + j * 128, 128, 128)],
            win.at[j, :, rows(k * 128, 128, 128)],
            wsem_in.at[j, k],
        )

    def wout_copy(j, k):
        return pltpu.make_async_copy(
            wout_hbm.at[rows(k * 384 + j * 128, 128, 128)],
            wout.at[j, rows(k * 128, 128, 128)],
            wsem_out.at[j, k],
        )

    for j in range(NC):

        @pl.loop(0, 8)
        def _(k):
            wout_copy(j, k).start()
            win_copy(j, k).start()

    loaded = []

    def need(copy, key, j):
        if (key, j) not in loaded:
            loaded.append((key, j))

            @pl.loop(0, 8)
            def _(k):
                copy(j, k).wait()

    barrier = pltpu.get_barrier_semaphore()
    for dev in (XR, XL, YR, YL, ZL, ZH, CO):
        pl.semaphore_signal(barrier, inc=1, device_id=dev, device_id_type=MESH)

    cg[0:2, 0] = cot[...].reshape(2, HALF, W)
    x = tok[...].astype(F32)
    lane = lax.broadcasted_iota(jnp.int32, (T, 128), 1)

    def two(a, b):
        return jnp.where(lane == 0, a, jnp.where(lane == 1, b, 0.0))

    stat[0] = two(jnp.sum(x, axis=1, keepdims=True), jnp.sum(x * x, axis=1, keepdims=True))
    pl.semaphore_wait(barrier, 7)

    def mean_inverse():
        mean = stat[4, :, 0:1] / MODEL_WIDTH
        return mean, lax.rsqrt(stat[4, :, 1:2] / MODEL_WIDTH - mean * mean + EPS)

    S = {}

    def spread(key, ref, first=0):
        own = slot(ref, 0, first)
        V[key] = [rc(own, slot(ref, 1, first), CO), rc(own, slot(ref, 2, first), ZL)]

    def spread_on(key, ref, first=0):
        recv(V[key][1])
        V[key].append(rc(slot(ref, 2, first), slot(ref, 3, first), CO))

    done = []

    def once(key, *cps):
        if key not in done:
            done.append(key)
            recv(*cps)

    def own_chip(key):
        once(key + "0", V[key][0])

    def whole(key):
        own_chip(key)
        once(key + "1", V[key][2])

    S["cotg"] = lambda: spread("cot", cg)
    S["cotf"] = lambda: spread_on("cot", cg)

    def st1():
        V["sa"] = rc(stat.at[0], stat.at[1], XA)

    def st2():
        recv(V["sa"])
        stat[2] = stat[0] + stat[1]
        V["sb"] = rc(stat.at[2], stat.at[3], XB)

    def st3():
        recv(V["sb"])
        stat[4] = stat[2] + stat[3]
        mean, inverse = mean_inverse()
        normed = ((tok[...].astype(F32) - mean) * inverse * gain[...]).astype(BF16)
        nf[0:2, 0] = normed.reshape(2, HALF, W)
        spread("nor", nf)

    S["st1"], S["st2"], S["st3"] = st1, st2, st3
    S["norf"] = lambda: spread_on("nor", nf)

    def coth():
        V["coth"] = rc(slot(cg, 0), slot(cg, 0, 4), ZH)

    def norh():
        V["norh"] = rc(
            nf.at[0:2, 0, :, rows((1 - zh) * FG, FG, 128)], slot(ngp, 0), ZH
        )

    def cph():
        recv(V["coth"])
        spread("cp", cg, 4)

    def nph():
        recv(V["norh"])
        spread("np", ngp)

    def ngt0():
        whole("nor")
        ngt[:, 0:G] = jnp.transpose(nf[:, :, :, rows(zh * FG, FG, 128)].reshape(G, FG))

    def ngt1():
        whole("np")
        ngt[:, G:] = jnp.transpose(ngp[...].reshape(G, FG))

    S["coth"], S["norh"], S["cph"], S["nph"] = coth, norh, cph, nph
    S["ngt0"], S["ngt1"] = ngt0, ngt1
    S["cpf"] = lambda: spread_on("cp", cg, 4)
    S["npf"] = lambda: spread_on("np", ngp)

    def add(part, buf):
        part[...] = (part[...].astype(F32) + buf[...].astype(F32)).astype(BF16)

    CA, CB = pl.ds(0, H // 2), pl.ds(H // 2, H // 2)

    def product(kind, j, h):
        key = "cot" if kind == 0 else "nor"
        (need(wout_copy, "o", j) if kind == 0 else need(win_copy, "i", j))
        own_chip(key) if h == 0 else whole(key)
        if j >= 2 and h != 1:
            drain(V["x1", kind, j - 2] + V["x2", kind, j - 2])
        src = cg if kind == 0 else nf
        part = px.at[kind, j % 2]

        @pl.loop(0, H // 256)
        def _(n):
            at = rows(n * 256, 256, 256)
            if h is None:
                left = src[0:4].reshape(G, W)
            else:
                left = src[0:4, h].reshape(G // 2, W)
            if kind == 0:
                out = lax.dot_general(left, wout[j, at], LAST, preferred_element_type=F32)
            else:
                out = jnp.dot(left, win[j, :, at], preferred_element_type=F32)
            if h is None:
                part[:, :, :, at] = out.astype(BF16).reshape(4, 2, HALF, 256)
            else:
                part[:, h, :, at] = out.astype(BF16).reshape(4, HALF, 256)

        buf = rx1.at[kind, j]
        if h is None:
            new = [rc(part.at[cq, 0], buf.at[0], XR), rc(part.at[cq, 1], buf.at[1], XL)]
        else:
            new = [
                rc(part.at[cq, h, :, CA], buf.at[h, :, CA], XR),
                rc(part.at[cq, h, :, CB], buf.at[h, :, CB], XL),
            ]
        V["x1", kind, j, h] = new
        V["x1", kind, j] = V.get(("x1", kind, j), []) + new

    def second(kind, j, h):
        one, other = V["x1", kind, j, h]
        part, buf, out = px.at[kind, j % 2], rx1.at[kind, j], rx2.at[kind, j]
        new = []
        if h is None:
            recv(one)
            add(part.at[cr, 0], buf.at[0])
            new.append(rc(part.at[cr], out.at[0], XR))
            recv(other)
            add(part.at[cl, 1], buf.at[1])
            new.append(rc(part.at[cl], out.at[1], XL))
        else:
            recv(one)
            add(part.at[cr, h, :, CA], buf.at[h, :, CA])
            new.append(rc(part.at[cr, h], out.at[0, h], XR))
            recv(other)
            add(part.at[cl, h, :, CB], buf.at[h, :, CB])
            new.append(rc(part.at[cl, h], out.at[1, h], XL))
        V["x2", kind, j] = V.get(("x2", kind, j), []) + new

    def activate(j):
        recv(*V["x2", 0, j], *V["x2", 1, j])

        @pl.loop(0, H // 256)
        def _(n):
            at = rows(n * 256, 256, 256)

            def total(kind):
                return (
                    px[kind, j % 2, c, :, :, at].astype(F32)
                    + rx2[kind, j, 0, :, :, at].astype(F32)
                    + rx2[kind, j, 1, :, :, at].astype(F32)
                ).reshape(T, 256)

            dact, pre = total(0), total(1)
            cdf = 0.5 * (1.0 + lax.erf(pre * 0.7071067811865476))
            dens = jnp.exp(-0.5 * pre * pre) * 0.3989422804014327
            ab[j, rows(c * T, T), at] = (pre * cdf).astype(BF16)
            dg[j, rows(c * T, T), at] = (dact * (cdf + pre * dens)).astype(BF16)

        both_ways(("a", j), ab.at[j], 0)

    def both_ways(key, ref, base):
        own = ref.at[rows(base + c * T, T)]
        V[key] = [rc(own, own, XR), rc(own, own, XL)]

    def forward(key, ref, base):
        one, other = V[key]
        once((key, 0), one)
        a = ref.at[rows(base + cl * T, HALF)]
        V[key].append(rc(a, a, XR))
        once((key, 1), other)
        b = ref.at[rows(base + cr * T + HALF, HALF)]
        V[key].append(rc(b, b, XL))

    def ends(key):
        once((key, 2), V[key][2])
        once((key, 3), V[key][3])

    def over_z(kind, j, piece):
        if kind == "a":
            return rc(
                ab.at[j, rows(piece * T, T), rows((1 - zh) * 512, 512, 128)],
                ag.at[j, rows(G + piece * T, T)],
                ZH,
            )
        return rc(dg.at[j, rows(piece * T, T)], dg.at[j, rows(G + piece * T, T)], ZH)

    def partner_steps(kind, j, way):
        ref = ag if kind == "a" else dg
        key = (kind + "p", j)
        name = "z%s%s%d"

        def z_own():
            V["z", kind, j] = over_z(kind, j, c)

        S["z%s%d" % (kind, j)] = z_own

        def over_x():
            once(("z", kind, j), V["z", kind, j])
            both_ways(key, ref.at[j], G)

        def opposite():
            ends((kind, j))
            V["zq", kind, j] = over_z(kind, j, cq)

        def neighbours():
            once(((kind, j), 0), V[kind, j][0])
            once(((kind, j), 1), V[kind, j][1])
            V["zn", kind, j] = [over_z(kind, j, cl), over_z(kind, j, cr)]

        if way < 4:
            S["%sp%d" % (kind, j)] = over_x
        if way == 1:
            S["%spf%d" % (kind, j)] = lambda: forward(key, ref.at[j], G)
        if way > 1:
            S[name % (kind, "q", j)] = opposite
        if way == 4:
            S[name % (kind, "n", j)] = neighbours

        def wait():
            if way == 1:
                ends(key)
            elif way == 2:
                recv(*V[key], V["zq", kind, j])
            else:
                recv(V["z", kind, j], *V["zn", kind, j], V["zq", kind, j])

        return wait

    ocps = []

    def out_copy(key, j, k):
        if key == "o":
            return pltpu.make_async_copy(
                go2.at[j, 0], gout_out.at[0, pl.ds(j * 128, 128)], osem.at[0, j, 0]
            )
        return pltpu.make_async_copy(
            gi2.at[j, 0, :, pl.ds(k * 128, 128)],
            gin_out.at[0, :, pl.ds(k * 384 + j * 128, 128)],
            osem.at[1, j, k],
        )

    def gradient_steps(key, j, wait, split):
        part, b1, b2, size = (
            (pgo.at[j % 2], go1.at[j], go2.at[j], 128)
            if key == "o"
            else (pgi.at[j % 2], gi1.at[j], gi2.at[j], FB)
        )
        pieces = (("a", 0), ("b", 1)) if split else (("", 0),)
        ps = size // len(pieces)
        h = ps // 2

        def block(b):
            if key == "o":
                at = rows(b * size, size, 128)
                part[at] = lax.dot_general(
                    ag[j, :, at], cg[...].reshape(2 * G, W), FIRST, preferred_element_type=F32
                ).astype(BF16)
            else:
                at = rows(b * size, size)
                part[at] = jnp.dot(ngt[at], dg[j], preferred_element_type=F32).astype(BF16)

        def compute():
            if key == "o":
                ends(("a", j))
                ag[j, 0:G] = ab[j, :, rows(zh * 512, 512, 128)]
                whole("cp")
            else:
                ends(("d", j))
            wait()
            if j >= 2:
                drain(V["y", key, j - 2])
            block(yq)
            V["y", key, j] = []
            for name, p in pieces:
                new = [
                    rc(part.at[rows(yq * size + p * ps, h)], b1.at[rows(2 * p * h, h)], YR),
                    rc(part.at[rows(yq * size + p * ps + h, h)], b1.at[rows(2 * p * h + h, h)], YL),
                ]
                V["y1", key, j, name] = new
                V["y", key, j] += new

            @pl.loop(1, 4)
            def _(i):
                block(lax.rem(yq + i, 4))

        S["g%s%d" % (key, j)] = compute

        def piece_steps(name, p):
            def on():
                one, other = V["y1", key, j, name]
                recv(one)
                add(part.at[rows(yr * size + p * ps, h)], b1.at[rows(2 * p * h, h)])
                new = [rc(part.at[rows(yr * size + p * ps, ps)], b2.at[0, rows(p * ps, ps)], YR)]
                recv(other)
                add(part.at[rows(yl * size + p * ps + h, h)], b1.at[rows(2 * p * h + h, h)])
                new.append(rc(part.at[rows(yl * size + p * ps, ps)], b2.at[1, rows(p * ps, ps)], YL))
                V["y2", key, j, name] = new
                V["y", key, j] += new

            def end():
                recv(*V["y2", key, j, name])
                at = rows(p * ps, ps)
                b2[0, at] = (
                    part[rows(y * size + p * ps, ps)].astype(F32)
                    + b2[0, at].astype(F32)
                    + b2[1, at].astype(F32)
                ).astype(BF16)
                if name != "a":
                    for k in range(1 if key == "o" else 8):
                        cp = out_copy(key, j, k)
                        cp.start()
                        ocps.append(cp)

            S["gs%s%d%s" % (key, j, name)] = on
            S["ge%s%d%s" % (key, j, name)] = end

        for name, p in pieces:
            piece_steps(name, p)

    def chunk_steps(j):
        for kind, name, k, split in (
            (0, "dact", "d", j in SPLIT_DACT),
            (1, "pre", "p", j in SPLIT_PRE),
        ):
            for h, tail in ((0, "a"), (1, "b")) if split else ((None, ""),):
                S["%s%d%s" % (name, j, tail)] = lambda kind=kind, h=h: product(kind, j, h)
                S["rs%s%d%s" % (k, j, tail)] = lambda kind=kind, h=h: second(kind, j, h)
        S["act%d" % j] = lambda: activate(j)
        S["sd%d" % j] = lambda: both_ways(("d", j), dg.at[j], 0)
        S["af%d" % j] = lambda: forward(("a", j), ab.at[j], 0)
        S["df%d" % j] = lambda: forward(("d", j), dg.at[j], 0)
        wait_a = partner_steps("a", j, ACT_WAY[j])
        wait_d = partner_steps("d", j, DPRE_WAY[j])
        gradient_steps("o", j, wait_a, j in SPLIT_OUT)
        gradient_steps("i", j, wait_d, j in SPLIT_IN)

    for j in range(NC):
        chunk_steps(j)

    def out():
        for j in range(NC):
            ends(("a", j))

        @pl.loop(0, W // 256)
        def _(n):
            at = rows(n * 256, 256, 256)
            total = jnp.dot(ab[0], wout[0, :, at], preferred_element_type=F32)
            for j in range(1, NC):
                total += jnp.dot(ab[j], wout[j, :, at], preferred_element_type=F32)
            po[0, :, :, :, at] = total.astype(BF16).reshape(4, 2, HALF, 256)

        V["lo1"] = rc(po.at[0, 2:4], ro1.at[0], CO)

    def dna():
        for j in (0, 1):
            ends(("d", j))

        @pl.loop(0, W // 256)
        def _(n):
            at = rows(n * 256, 256, 256)
            acc[:, at] = sum(
                lax.dot_general(dg[j, 0:G], win[j, at], LAST, preferred_element_type=F32)
                for j in (0, 1)
            )

    def dnb():
        ends(("d", 2))

        @pl.loop(0, W // 256)
        def _(n):
            at = rows(n * 256, 256, 256)
            total = acc[:, at] + lax.dot_general(
                dg[2, 0:G], win[2, at], LAST, preferred_element_type=F32
            )
            po[1, :, :, :, at] = total.astype(BF16).reshape(4, 2, HALF, 256)

        V["dn1"] = rc(po.at[1, 2:4], ro1.at[1], CO)

    def row_second(q, key):
        recv(V[key])
        add(po.at[q, 0:2, 1], ro1.at[q, :, 1])
        return rc(po.at[q, 0:2, 1], ro2.at[q], ZL)

    def row_sum(q):
        return (
            po[q, 0:2, 0].astype(F32) + ro1[q, :, 0].astype(F32) + ro2[q].astype(F32)
        ).reshape(T, W)

    def lo2():
        V["lo2"] = row_second(0, "lo1")

    def dn2():
        V["dn2"] = row_second(1, "dn1")

    def lo3():
        recv(V["lo2"])
        layer_out[...] = (tok[...].astype(F32) + row_sum(0)).astype(BF16)

    def fin():
        recv(V["dn2"])
        mean, inverse = mean_inverse()
        dnorm = row_sum(1)
        xhat = (tok[...].astype(F32) - mean) * inverse
        gains[0] = jnp.sum((dnorm * xhat).reshape(T // 8, 8, W), axis=0)
        V["ga"] = rc(gains.at[0], gains.at[1], CO)
        dxhat = dnorm * gain[...]
        tails[0] = two(
            jnp.sum(dxhat, axis=1, keepdims=True), jnp.sum(dxhat * xhat, axis=1, keepdims=True)
        )
        V["ta"] = rc(tails.at[0], tails.at[1], XA)

    def t2():
        recv(V["ta"])
        tails[2] = tails[0] + tails[1]
        V["tb"] = rc(tails.at[2], tails.at[3], XB)

    def t3():
        recv(V["tb"])
        tails[4] = tails[2] + tails[3]
        mean, inverse = mean_inverse()
        first = tails[4, :, 0:1] / MODEL_WIDTH
        second = tails[4, :, 1:2] / MODEL_WIDTH
        xhat = (tok[...].astype(F32) - mean) * inverse
        token_grad[...] = (
            cot[...].astype(F32) + inverse * (row_sum(1) * gain[...] - first - xhat * second)
        ).astype(BF16)

    def gain_step(i, old, new, dev):
        def step():
            recv(V[old])
            gains[2 * i + 2] = gains[2 * i] + gains[2 * i + 1]
            V[new] = rc(gains.at[2 * i + 2], gains.at[2 * i + 3], dev)

        return step

    def gz():
        recv(V["ge"])
        gain_grad[...] = jnp.sum(gains[8] + gains[9], axis=0, keepdims=True)

    S.update(out=out, dna=dna, dnb=dnb, lo2=lo2, dn2=dn2, lo3=lo3, fin=fin, t2=t2, t3=t3, gz=gz)
    S["gb"] = gain_step(0, "ga", "gb", ZL)
    S["gc"] = gain_step(1, "gb", "gc", ZH)
    S["gd"] = gain_step(2, "gc", "gd", YA)
    S["ge"] = gain_step(3, "gd", "ge", YB)

    assert sorted(S) == sorted(ORDER)
    for name in ORDER:
        S[name]()
    drain(list(sends))
    for cp in ocps:
        cp.wait()
    assert count[0] <= N_COPIES, count[0]


N_COPIES = 180


def body(tokens, norm_scale_gain, in_weight, out_weight, cotangent):
    vm = pl.BlockSpec(memory_space=pltpu.VMEM)
    hbm = pl.BlockSpec(memory_space=pl.ANY)
    layer_out, token_grad, gain_grad, grad_in, grad_out = pl.pallas_call(
        kernel,
        out_shape=(
            jax.ShapeDtypeStruct((T, W), BF16),
            jax.ShapeDtypeStruct((T, W), BF16),
            jax.ShapeDtypeStruct((1, W), F32),
            jax.ShapeDtypeStruct((1, FB, NC * H), BF16),
            jax.ShapeDtypeStruct((1, NC * 128, W), BF16),
        ),
        in_specs=[vm, vm, hbm, hbm, vm],
        out_specs=(vm, vm, vm, hbm, hbm),
        scratch_shapes=[
            pltpu.VMEM((NC, W, H), BF16),
            pltpu.VMEM((NC, H, W), BF16),
            pltpu.VMEM((4, 2, HALF, W), BF16),
            pltpu.VMEM((4, 2, HALF, FG), BF16),
            pltpu.VMEM((FG, 2 * G), BF16),
            pltpu.VMEM((8, 2, HALF, W), BF16),
            pltpu.VMEM((NC, G, H), BF16),
            pltpu.VMEM((NC, 2 * G, 512), BF16),
            pltpu.VMEM((NC, 2 * G, H), BF16),
            pltpu.VMEM((2, 2, 4, 2, HALF, H), BF16),
            pltpu.VMEM((2, NC, 2, HALF, H), BF16),
            pltpu.VMEM((2, NC, 2, 2, HALF, H), BF16),
            pltpu.VMEM((2, 4, 2, HALF, W), BF16),
            pltpu.VMEM((2, 2, 2, HALF, W), BF16),
            pltpu.VMEM((2, 2, HALF, W), BF16),
            pltpu.VMEM((G, W), F32),
            pltpu.VMEM((2, FG, H), BF16),
            pltpu.VMEM((2, 512, W), BF16),
            pltpu.VMEM((NC, FB, H), BF16),
            pltpu.VMEM((NC, 2, FB, H), BF16),
            pltpu.VMEM((NC, 128, W), BF16),
            pltpu.VMEM((NC, 2, 128, W), BF16),
            pltpu.VMEM((5, T, 128), F32),
            pltpu.VMEM((5, T, 128), F32),
            pltpu.VMEM((10, 8, W), F32),
            pltpu.SemaphoreType.DMA((NC, 8)),
            pltpu.SemaphoreType.DMA((NC, 8)),
            pltpu.SemaphoreType.DMA((2, NC, 8)),
            pltpu.SemaphoreType.DMA((N_COPIES,)),
            pltpu.SemaphoreType.DMA((N_COPIES,)),
        ],
        compiler_params=pltpu.CompilerParams(
            collective_id=0, has_side_effects=True, vmem_limit_bytes=63 * 2**20
        ),
        cost_estimate=pl.CostEstimate(
            flops=22 * 10**9, bytes_accessed=24 * 10**6, transcendentals=600000
        ),
        name="feed_forward",
    )(tokens, norm_scale_gain.reshape(1, W), in_weight, out_weight, cotangent)
    return (layer_out, token_grad, gain_grad.reshape(W), grad_in, grad_out)


def solution(mesh):
    in_specs = (
        P(("dp", "row"), "col"),
        P("col"),
        P("col", "row"),
        P("row", "col"),
        P(("dp", "row"), "col"),
    )
    out_specs = (
        P(("dp", "row"), "col"),
        P(("dp", "row"), "col"),
        P("col"),
        P("dp", "col", "row"),
        P("dp", "row", "col"),
    )
    return jax.shard_map(body, mesh=mesh, in_specs=in_specs, out_specs=out_specs, check_vma=False)
```

time: 525 us -> 159 us (0.30)
  waiting for transfers between devices: 359 us -> 0 us
  Pallas kernels: 0 us -> 149 us
  blocking collectives: 83.7 us -> 0 us
  matrix products: 52.3 us -> 0 us
  between operations: 14.2 us -> 0.65 us
  other arithmetic: 11.6 us -> 1.41 us
    reduce_scatter x6 -> x0, waiting for transfers between devices: 261 us -> none  [the longest x1 128 us: body(): lax.psum_scatter(lax.dot_general(columns, cot_full, CONTRACT_FIRST, prefe...]
    pallas_call x0 -> x1, Pallas kernels: none -> 149 us  [body(): pl.pallas_call(kernel, out_shape=(jax.ShapeDtypeStruct((T, W), BF16), jax...]
    all_gather x4 -> x0, waiting for transfers between devices: 96.4 us -> none  [the longest x1 32.2 us: body(): lax.all_gather((dact * gelu_slope(pre)).astype(jnp.bfloat16), 'col', axis...]
    psum x3 -> x0, blocking collectives: 83.7 us -> none  [the longest x1 67.9 us: body(): lax.psum(jnp.sum(normed_cotangent * centered_input, axis=0), ('dp', 'row'))]
    dot_general x6 -> x0, matrix products: 52.3 us -> none  [the longest x1 9.39 us: body(): jnp.dot(block, out_weight, preferred_element_type=jnp.float32)]
    convert_element_type x3 -> x0, other arithmetic: 9.06 us -> none  [the longest x1 4.91 us: body(): (dact * gelu_slope(pre)).astype(jnp.bfloat16)]
  transfers between devices with their start and end apart: 10 -> 0, of which waited for: 8 -> 0; matrix products, arithmetic and copies ran while one was open for 11% -> 0% of each run, Pallas kernels for 0% -> 0%
where the time goes in v2:
time: 159 us
  Pallas kernels  149 us (94%)
  local copies, waits for them, and re-layouts  7.39 us (5%)
    pallas_call x1, Pallas kernels, body(): pl.pallas_call(kernel, out_shape=(jax.ShapeDtypeStruct((T, W), BF16), jax...  149 us
    unnamed x8, local copies, waits for them, and re-layouts  6.1 us

profile of v2, /device:TPU:1, one launch (start us, length us, event | category | flops | bytes accessed | tf_op | source)
XLA Modules:
  0.0 158.6 jit_solution(10795417018604009897)
XLA Ops:
  0.6 1.3 reshape.16.gain
  1.9 149.2 %feed_forward.1 = (bf16[96,1536]{1,0:T(8,128)(2,1)}, bf16[96,1536]{1,0:T(8,128)(2,1)}, f32[1,1536]{1,0:T(1,128)}, bf16[1,192,3072]{2,1,0:T(8,128)(2,1)}, bf16[1,384,1536]{2,1,0:T(8,128)(2,1)}) custom-call(bf16[96,1536]{1,0:T(8,128)(2,1)} %tok.1, f32[1,1536]{1,0:T(1,128)} %reshape.16.gain, bf16[1536,3072]{1,0:T(8,128)(2,1)} %win_hbm.1, ...), custom_call_target="tpu_custom_call" | custom-call | flops 22000001024 | bytes 24000000 | tf_op jit(solution)/shard_map/feed_forward/pallas_call | solution.py:603
  151.1 0.0 copy-start.1
  151.1 1.4 reduce
  152.5 1.7 %copy.14 = bf16[96,1536]{1,0:T(8,128)(2,1)} copy(bf16[96,1536]{1,0:T(8,128)(2,1)} %get-tuple-element.20) | data formatting | bytes 589824
  154.2 1.7 %copy.15 = bf16[96,1536]{1,0:T(8,128)(2,1)} copy(bf16[96,1536]{1,0:T(8,128)(2,1)} %get-tuple-element.21) | data formatting | bytes 589824
  155.9 0.0 copy-done.1
  155.9 0.0 copy-start
  155.9 1.0 copy.16
  156.9 0.7 copy-done
  157.6 1.0 copy.17
Async XLA Ops:
  151.1 4.8 %copy-start.1 = (bf16[1,192,3072]{2,1,0:T(8,128)(2,1)S(1)}, bf16[1,192,3072]{2,1,0:T(8,128)(2,1)}, u32[]{:S(2)}) copy-start(bf16[1,192,3072]{2,1,0:T(8,128)(2,1)} %get-tuple-element.23) | copy-start | bytes 3538948
  155.9 1.7 %copy-start = (bf16[1,384,1536]{2,1,0:T(8,128)(2,1)S(1)}, bf16[1,384,1536]{2,1,0:T(8,128)(2,1)}, u32[]{:S(2)}) copy-start(bf16[1,384,1536]{2,1,0:T(8,128)(2,1)} %get-tuple-element.24) | copy-start | bytes 3538948

commit v3 on v2

--- a/solution.py
+++ b/solution.py
@@ -23,21 +23,23 @@
 FIRST = (((0,), (0,)), ((), ()))
 
 ACT_WAY = (2, 2, 2)
-DPRE_WAY = (2, 2, 2)
+DPRE_WAY = (4, 2, 2)
 SPLIT_DACT = (0, 1)
 SPLIT_PRE = (0,)
-SPLIT_IN = (2,)
-SPLIT_OUT = ()
+SPLIT_IN = (0, 2)
+SPLIT_OUT = (2,)
+SPLIT_ACT = (0,)
 
 ORDER = (
-    "cotg", "st1", "dact1a", "st2", "dact0a", "rsd1a", "st3", "coth", "rsd0a", "cotf", "dact1b",
-    "dact0b", "pre0a", "rsd1b", "norf", "rsd0b", "pre0b", "rsp0a", "pre1", "cph", "rsp0b", "rsp1",
-    "norh", "act0", "dact2", "af0", "cpf", "sd0", "za0", "nph", "ap0", "act1", "npf", "zaq0",
-    "ngt0", "df0", "zd0", "sd1", "go0", "pre2", "zdq0", "dp0", "ngt1", "gso0", "af1", "zd1", "df1",
-    "rsp2", "rsd2", "gi0", "za1", "ap1", "dp1", "gsi0", "zaq1", "zdq1", "act2", "go1", "za2",
-    "zd2", "gi1", "sd2", "gso1", "dna", "gsi1", "af2", "geo0", "df2", "zaq2", "ap2", "dnb", "go2",
-    "dp2", "zdq2", "dn2", "out", "gei0", "gei1", "gi2", "gso2", "gsi2a", "fin", "gb", "gc", "lo2",
-    "gd", "geo1", "gsi2b", "t2", "geo2", "lo3", "gei2a", "ge", "t3", "gei2b", "gz",
+    "cotz", "cotc", "st1", "dact0a", "dact1a", "st3", "rsd0a", "coth", "rsd1a", "cotf", "pre0a",
+    "norh", "dact1b", "dact0b", "rsp0a", "norf", "rsd0b", "pre0b", "act0a", "rsp0b", "dgr0a",
+    "cph", "af0a", "act0b", "pre2", "za0", "nph", "af0b", "dgr0b", "df0a", "zaq0", "zd0", "ap0",
+    "pre1", "rsp2", "cpf", "zdn0", "df0b", "go0", "npf", "rsp1", "ngt1", "gso0", "act2", "zdq0",
+    "ngt0", "za2", "act1", "af2", "gi0", "af1", "gsi0a", "ap2", "geo0", "za1", "dact2", "zaq2",
+    "zaq1", "gsi0b", "rsd1b", "ap1", "gei0a", "rsd2", "go2", "dgr1", "go1", "gso2b", "zd1",
+    "gso2a", "dgr2", "out", "df1", "zd2", "gso1", "df2", "gei0b", "zdq1", "dp1", "dna", "zdq2",
+    "dp2", "dnb", "gi1", "dn2", "geo2b", "gi2", "gsi2a", "geo1", "fin", "gsi1", "gb", "gc",
+    "gei2a", "lo2", "gd", "geo2a", "gsi2b", "gei1", "ge", "t3", "lo3", "gei2b", "gz",
 )
 
 
@@ -48,7 +50,7 @@
 def kernel(
     tok, gain, win_hbm, wout_hbm, cot,
     layer_out, token_grad, gain_grad, gin_out, gout_out,
-    win, wout, nf, ngp, ngt, cg, ab, ag, dg, px, rx1, rx2, po, ro1, ro2, acc,
+    win, wout, nf, ngp, ngt, cg, ab, ag, dg, px, rx1, rx2, po, ro1, ro2, acc, slope,
     pgi, pgo, gi1, gi2, go1, go2, stat, tails, gains, wsem_in, wsem_out, osem, ssem, rsem,
 ):
     d, r, c = lax.axis_index("dp"), lax.axis_index("row"), lax.axis_index("col")
@@ -57,12 +59,10 @@
     cr, cl = lax.rem(c + 1, 4), lax.rem(c + 3, 4)
     yr, yl = lax.rem(y + 1, 4), lax.rem(y + 3, 4)
     cq, yq = lax.rem(c + 2, 4), lax.rem(y + 2, 4)
-    XR, XL = (d, r, cr), (d, r, cl)
+    XR, XL, XQ = (d, r, cr), (d, r, cl), (d, r, cq)
     YR, YL = (zh * 4 + yr, r, c), (zh * 4 + yl, r, c)
     ZL, ZH = (d, (1 - zl) * 2 + co, c), ((1 - zh) * 4 + y, r, c)
     CO = (d, zl * 2 + 1 - co, c)
-    XA = (d, r, c + 1 - 2 * lax.rem(c, 2))
-    XB = (d, r, 3 - c)
     YA = (zh * 4 + y + 1 - 2 * lax.rem(y, 2), r, c)
     YB = (zh * 4 + 3 - y, r, c)
 
@@ -71,7 +71,7 @@
 
     count = [0]
     sends = []
-    V = {}
+    V = {"cot": {}}
 
     def rc(src, dst, dev):
         i = count[0]
@@ -125,7 +125,7 @@
                 copy(j, k).wait()
 
     barrier = pltpu.get_barrier_semaphore()
-    for dev in (XR, XL, YR, YL, ZL, ZH, CO):
+    for dev in (XR, XL, XQ, YR, YL, ZL, ZH, CO):
         pl.semaphore_signal(barrier, inc=1, device_id=dev, device_id_type=MESH)
 
     cg[0:2, 0] = cot[...].reshape(2, HALF, W)
@@ -136,7 +136,7 @@
         return jnp.where(lane == 0, a, jnp.where(lane == 1, b, 0.0))
 
     stat[0] = two(jnp.sum(x, axis=1, keepdims=True), jnp.sum(x * x, axis=1, keepdims=True))
-    pl.semaphore_wait(barrier, 7)
+    pl.semaphore_wait(barrier, 8)
 
     def mean_inverse():
         mean = stat[4, :, 0:1] / MODEL_WIDTH
@@ -146,11 +146,11 @@
 
     def spread(key, ref, first=0):
         own = slot(ref, 0, first)
-        V[key] = [rc(own, slot(ref, 1, first), CO), rc(own, slot(ref, 2, first), ZL)]
+        V[key] = {0: rc(own, slot(ref, 1, first), CO), 1: rc(own, slot(ref, 2, first), ZL)}
 
     def spread_on(key, ref, first=0):
         recv(V[key][1])
-        V[key].append(rc(slot(ref, 2, first), slot(ref, 3, first), CO))
+        V[key][2] = rc(slot(ref, 2, first), slot(ref, 3, first), CO)
 
     done = []
 
@@ -166,26 +166,33 @@
         own_chip(key)
         once(key + "1", V[key][2])
 
-    S["cotg"] = lambda: spread("cot", cg)
+    def cotc():
+        V["cot"][0] = rc(slot(cg, 0), slot(cg, 1), CO)
+
+    def cotz():
+        V["cot"][1] = rc(slot(cg, 0), slot(cg, 2), ZL)
+
+    S["cotc"], S["cotz"] = cotc, cotz
     S["cotf"] = lambda: spread_on("cot", cg)
 
+    def to_column(key, ref):
+        V[key] = [rc(ref.at[0], ref.at[1 + i], dev) for i, dev in enumerate((XR, XL, XQ))]
+
+    def of_column(key, ref):
+        recv(*V[key])
+        ref[4] = (ref[0] + ref[3]) + (ref[1] + ref[2])
+
     def st1():
-        V["sa"] = rc(stat.at[0], stat.at[1], XA)
-
-    def st2():
-        recv(V["sa"])
-        stat[2] = stat[0] + stat[1]
-        V["sb"] = rc(stat.at[2], stat.at[3], XB)
+        to_column("sa", stat)
 
     def st3():
-        recv(V["sb"])
-        stat[4] = stat[2] + stat[3]
+        of_column("sa", stat)
         mean, inverse = mean_inverse()
-        normed = ((tok[...].astype(F32) - mean) * inverse * gain[...]).astype(BF16)
+        normed = ((tok[...].astype(F32) - mean) * inverse * gain[...].reshape(1, W)).astype(BF16)
         nf[0:2, 0] = normed.reshape(2, HALF, W)
         spread("nor", nf)
 
-    S["st1"], S["st2"], S["st3"] = st1, st2, st3
+    S["st1"], S["st3"] = st1, st3
     S["norf"] = lambda: spread_on("nor", nf)
 
     def coth():
@@ -276,46 +283,78 @@
             recv(other)
             add(part.at[cl, h, :, CB], buf.at[h, :, CB])
             new.append(rc(part.at[cl, h], out.at[1, h], XL))
+        V["x2", kind, j, h] = new
         V["x2", kind, j] = V.get(("x2", kind, j), []) + new
 
-    def activate(j):
-        recv(*V["x2", 0, j], *V["x2", 1, j])
+    def total(kind, j, h, at):
+        here = slice(None) if h is None else h
+        return (
+            px[kind, j % 2, c, here, :, at].astype(F32)
+            + rx2[kind, j, 0, here, :, at].astype(F32)
+            + rx2[kind, j, 1, here, :, at].astype(F32)
+        ).reshape(T if h is None else HALF, 256)
+
+    def arrived(kind, j, h):
+        split = j in (SPLIT_DACT, SPLIT_PRE)[kind]
+        for part in ((0, 1) if h is None else (h,)) if split else (None,):
+            once(("x2", kind, j, part), *V["x2", kind, j, part])
+
+    def own_rows(h):
+        return rows(c * T, T) if h is None else rows(c * T + h * HALF, HALF)
+
+    def activate(j, h):
+        arrived(1, j, h)
+        to = slice(0, T) if h is None else slice(h * HALF, (h + 1) * HALF)
 
         @pl.loop(0, H // 256)
         def _(n):
             at = rows(n * 256, 256, 256)
-
-            def total(kind):
-                return (
-                    px[kind, j % 2, c, :, :, at].astype(F32)
-                    + rx2[kind, j, 0, :, :, at].astype(F32)
-                    + rx2[kind, j, 1, :, :, at].astype(F32)
-                ).reshape(T, 256)
-
-            dact, pre = total(0), total(1)
+            pre = total(1, j, h, at)
             cdf = 0.5 * (1.0 + lax.erf(pre * 0.7071067811865476))
             dens = jnp.exp(-0.5 * pre * pre) * 0.3989422804014327
-            ab[j, rows(c * T, T), at] = (pre * cdf).astype(BF16)
-            dg[j, rows(c * T, T), at] = (dact * (cdf + pre * dens)).astype(BF16)
-
-        both_ways(("a", j), ab.at[j], 0)
-
-    def both_ways(key, ref, base):
-        own = ref.at[rows(base + c * T, T)]
+            ab[j, own_rows(h), at] = (pre * cdf).astype(BF16)
+            slope[j % 2, to, at] = cdf + pre * dens
+
+        both_ways(("a", j, h), ab.at[j], 0, h)
+
+    def dgelu(j, h):
+        arrived(0, j, h)
+        to = slice(0, T) if h is None else slice(h * HALF, (h + 1) * HALF)
+
+        @pl.loop(0, H // 256)
+        def _(n):
+            at = rows(n * 256, 256, 256)
+            dg[j, own_rows(h), at] = (total(0, j, h, at) * slope[j % 2, to, at]).astype(BF16)
+
+        both_ways(("d", j, h), dg.at[j], 0, h)
+
+    def both_ways(key, ref, base, h=None):
+        own = ref.at[rows(base + c * T, T) if h is None else rows(base + c * T + h * HALF, HALF)]
         V[key] = [rc(own, own, XR), rc(own, own, XL)]
 
-    def forward(key, ref, base):
+    def forward(key, ref, base, h=None):
         one, other = V[key]
         once((key, 0), one)
-        a = ref.at[rows(base + cl * T, HALF)]
+        if h is None:
+            a = ref.at[rows(base + cl * T, HALF)]
+            b = ref.at[rows(base + cr * T + HALF, HALF)]
+        else:
+            a = ref.at[rows(base + cl * T + h * HALF, HALF), CA]
+            b = ref.at[rows(base + cr * T + h * HALF, HALF), CB]
         V[key].append(rc(a, a, XR))
         once((key, 1), other)
-        b = ref.at[rows(base + cr * T + HALF, HALF)]
         V[key].append(rc(b, b, XL))
 
     def ends(key):
         once((key, 2), V[key][2])
         once((key, 3), V[key][3])
+
+    def halves(j):
+        return ((0, "a"), (1, "b")) if j in SPLIT_ACT else ((None, ""),)
+
+    def all_ends(kind, j):
+        for h, _ in halves(j):
+            ends((kind, j, h))
 
     def over_z(kind, j, piece):
         if kind == "a":
@@ -341,12 +380,13 @@
             both_ways(key, ref.at[j], G)
 
         def opposite():
-            ends((kind, j))
+            all_ends(kind, j)
             V["zq", kind, j] = over_z(kind, j, cq)
 
         def neighbours():
-            once(((kind, j), 0), V[kind, j][0])
-            once(((kind, j), 1), V[kind, j][1])
+            for h, _ in halves(j):
+                for i in (0, 1):
+                    once(((kind, j, h), i), V[kind, j, h][i])
             V["zn", kind, j] = [over_z(kind, j, cl), over_z(kind, j, cr)]
 
         if way < 4:
@@ -403,11 +443,11 @@
 
         def compute():
             if key == "o":
-                ends(("a", j))
+                all_ends("a", j)
                 ag[j, 0:G] = ab[j, :, rows(zh * 512, 512, 128)]
                 whole("cp")
             else:
-                ends(("d", j))
+                all_ends("d", j)
             wait()
             if j >= 2:
                 drain(V["y", key, j - 2])
@@ -447,7 +487,8 @@
                     + b2[0, at].astype(F32)
                     + b2[1, at].astype(F32)
                 ).astype(BF16)
-                if name != "a":
+                V["left", key, j] = V.get(("left", key, j), len(pieces)) - 1
+                if V["left", key, j] == 0:
                     for k in range(1 if key == "o" else 8):
                         cp = out_copy(key, j, k)
                         cp.start()
@@ -467,10 +508,11 @@
             for h, tail in ((0, "a"), (1, "b")) if split else ((None, ""),):
                 S["%s%d%s" % (name, j, tail)] = lambda kind=kind, h=h: product(kind, j, h)
                 S["rs%s%d%s" % (k, j, tail)] = lambda kind=kind, h=h: second(kind, j, h)
-        S["act%d" % j] = lambda: activate(j)
-        S["sd%d" % j] = lambda: both_ways(("d", j), dg.at[j], 0)
-        S["af%d" % j] = lambda: forward(("a", j), ab.at[j], 0)
-        S["df%d" % j] = lambda: forward(("d", j), dg.at[j], 0)
+        for h, tail in halves(j):
+            S["act%d%s" % (j, tail)] = lambda h=h: activate(j, h)
+            S["dgr%d%s" % (j, tail)] = lambda h=h: dgelu(j, h)
+            S["af%d%s" % (j, tail)] = lambda h=h: forward(("a", j, h), ab.at[j], 0, h)
+            S["df%d%s" % (j, tail)] = lambda h=h: forward(("d", j, h), dg.at[j], 0, h)
         wait_a = partner_steps("a", j, ACT_WAY[j])
         wait_d = partner_steps("d", j, DPRE_WAY[j])
         gradient_steps("o", j, wait_a, j in SPLIT_OUT)
@@ -481,7 +523,7 @@
 
     def out():
         for j in range(NC):
-            ends(("a", j))
+            all_ends("a", j)
 
         @pl.loop(0, W // 256)
         def _(n):
@@ -495,7 +537,7 @@
 
     def dna():
         for j in (0, 1):
-            ends(("d", j))
+            all_ends("d", j)
 
         @pl.loop(0, W // 256)
         def _(n):
@@ -506,7 +548,7 @@
             )
 
     def dnb():
-        ends(("d", 2))
+        all_ends("d", 2)
 
         @pl.loop(0, W // 256)
         def _(n):
@@ -545,26 +587,20 @@
         xhat = (tok[...].astype(F32) - mean) * inverse
         gains[0] = jnp.sum((dnorm * xhat).reshape(T // 8, 8, W), axis=0)
         V["ga"] = rc(gains.at[0], gains.at[1], CO)
-        dxhat = dnorm * gain[...]
+        dxhat = dnorm * gain[...].reshape(1, W)
         tails[0] = two(
             jnp.sum(dxhat, axis=1, keepdims=True), jnp.sum(dxhat * xhat, axis=1, keepdims=True)
         )
-        V["ta"] = rc(tails.at[0], tails.at[1], XA)
-
-    def t2():
-        recv(V["ta"])
-        tails[2] = tails[0] + tails[1]
-        V["tb"] = rc(tails.at[2], tails.at[3], XB)
+        to_column("ta", tails)
 
     def t3():
-        recv(V["tb"])
-        tails[4] = tails[2] + tails[3]
+        of_column("ta", tails)
         mean, inverse = mean_inverse()
         first = tails[4, :, 0:1] / MODEL_WIDTH
         second = tails[4, :, 1:2] / MODEL_WIDTH
         xhat = (tok[...].astype(F32) - mean) * inverse
         token_grad[...] = (
-            cot[...].astype(F32) + inverse * (row_sum(1) * gain[...] - first - xhat * second)
+            cot[...].astype(F32) + inverse * (row_sum(1) * gain[...].reshape(1, W) - first - xhat * second)
         ).astype(BF16)
 
     def gain_step(i, old, new, dev):
@@ -577,9 +613,9 @@
 
     def gz():
         recv(V["ge"])
-        gain_grad[...] = jnp.sum(gains[8] + gains[9], axis=0, keepdims=True)
-
-    S.update(out=out, dna=dna, dnb=dnb, lo2=lo2, dn2=dn2, lo3=lo3, fin=fin, t2=t2, t3=t3, gz=gz)
+        gain_grad[...] = jnp.sum(gains[8] + gains[9], axis=0)
+
+    S.update(out=out, dna=dna, dnb=dnb, lo2=lo2, dn2=dn2, lo3=lo3, fin=fin, t3=t3, gz=gz)
     S["gb"] = gain_step(0, "ga", "gb", ZL)
     S["gc"] = gain_step(1, "gb", "gc", ZH)
     S["gd"] = gain_step(2, "gc", "gd", YA)
@@ -594,7 +630,20 @@
     assert count[0] <= N_COPIES, count[0]
 
 
-N_COPIES = 180
+N_COPIES = 230
+
+
+def copy_kernel(*refs):
+    src, dst, via, (one, two) = refs[:5], refs[5:10], refs[10:15], refs[15:]
+    first = [pltpu.make_async_copy(src[i], via[i], one.at[i]) for i in range(5)]
+    then = [pltpu.make_async_copy(via[i], dst[i], two.at[i]) for i in range(5)]
+    for cp in first:
+        cp.start()
+    for a, b in zip(first, then):
+        a.wait()
+        b.start()
+    for cp in then:
+        cp.wait()
 
 
 def body(tokens, norm_scale_gain, in_weight, out_weight, cotangent):
@@ -605,7 +654,7 @@
         out_shape=(
             jax.ShapeDtypeStruct((T, W), BF16),
             jax.ShapeDtypeStruct((T, W), BF16),
-            jax.ShapeDtypeStruct((1, W), F32),
+            jax.ShapeDtypeStruct((W,), F32),
             jax.ShapeDtypeStruct((1, FB, NC * H), BF16),
             jax.ShapeDtypeStruct((1, NC * 128, W), BF16),
         ),
@@ -628,6 +677,7 @@
             pltpu.VMEM((2, 2, 2, HALF, W), BF16),
             pltpu.VMEM((2, 2, HALF, W), BF16),
             pltpu.VMEM((G, W), F32),
+            pltpu.VMEM((2, T, H), F32),
             pltpu.VMEM((2, FG, H), BF16),
             pltpu.VMEM((2, 512, W), BF16),
             pltpu.VMEM((NC, FB, H), BF16),
@@ -650,8 +700,17 @@
             flops=22 * 10**9, bytes_accessed=24 * 10**6, transcendentals=600000
         ),
         name="feed_forward",
-    )(tokens, norm_scale_gain.reshape(1, W), in_weight, out_weight, cotangent)
-    return (layer_out, token_grad, gain_grad.reshape(W), grad_in, grad_out)
+    )(tokens, norm_scale_gain, in_weight, out_weight, cotangent)
+    arrays = (layer_out, token_grad, gain_grad, grad_in, grad_out)
+    return pl.pallas_call(
+        copy_kernel,
+        out_shape=tuple(jax.ShapeDtypeStruct(a.shape, a.dtype) for a in arrays),
+        in_specs=[hbm] * 5,
+        out_specs=(hbm,) * 5,
+        scratch_shapes=[pltpu.VMEM(a.shape, a.dtype) for a in arrays]
+        + [pltpu.SemaphoreType.DMA((5,)), pltpu.SemaphoreType.DMA((5,))],
+        name="results",
+    )(*arrays)
 
 
 def solution(mesh):

time: 159 us -> 142 us (0.89)
  Pallas kernels: 149 us -> 141 us
  local copies, waits for them, and re-layouts: 7.39 us -> 0 us
    pallas_call x1, Pallas kernels: 149 us -> 138 us  [body(): pl.pallas_call(kernel, out_shape=(jax.ShapeDtypeStruct((T, W), BF16), jax...]
    unnamed x8 -> x0, local copies, waits for them, and re-layouts: 6.1 us -> none
    pallas_call x0 -> x1, Pallas kernels: none -> 2.97 us  [body(): pl.pallas_call(copy_kernel, out_shape=tuple((jax.ShapeDtypeStruct(a.shape...]
where the time goes in v3:
time: 142 us; the launch traced here: 141 us
  Pallas kernels  141 us (99%)
    pallas_call x1, Pallas kernels, body(): pl.pallas_call(kernel, out_shape=(jax.ShapeDtypeStruct((T, W), BF16), jax...  138 us
    pallas_call x1, Pallas kernels, body(): pl.pallas_call(copy_kernel, out_shape=tuple((jax.ShapeDtypeStruct(a.shape...  2.97 us

profile of v3, /device:TPU:1, one launch (start us, length us, event | category | flops | bytes accessed | tf_op | source)
XLA Modules:
  0.0 141.3 jit_solution(4477051600600381321)
XLA Ops:
  0.6 137.6 %feed_forward.1 = (bf16[96,1536]{1,0:T(8,128)(2,1)}, bf16[96,1536]{1,0:T(8,128)(2,1)}, f32[1536]{0:T(1024)}, bf16[1,192,3072]{2,1,0:T(8,128)(2,1)}, bf16[1,384,1536]{2,1,0:T(8,128)(2,1)}) custom-call(bf16[96,1536]{1,0:T(8,128)(2,1)} %tok.1, f32[1536]{0:T(1024)} %gain.1, bf16[1536,3072]{1,0:T(8,128)(2,1)} %win_hbm.1, bf16[3072,1536]{1,0:T(8,128)(2,1)} %wout_hbm.1, ...), custom_call_target="tpu_custom_call" | custom-call | flops 22000001024 | bytes 24000000 | tf_op jit(solution)/shard_map/feed_forward/pallas_call | solution.py:652
  138.2 3.0 %results.1 = (bf16[96,1536]{1,0:T(8,128)(2,1)}, bf16[96,1536]{1,0:T(8,128)(2,1)}, f32[1536]{0:T(1024)}, bf16[1,192,3072]{2,1,0:T(8,128)(2,1)}, bf16[1,384,1536]{2,1,0:T(8,128)(2,1)}) custom-call(bf16[96,1536]{1,0:T(8,128)(2,1)} %get-tuple-element.10.refs_0_, bf16[96,1536]{1,0:T(8,128)(2,1)} %get-tuple-element.11.refs_1_, f32[1536]{0:T(1024)} %get-tuple-element.12.refs_2_, ...), custom_call_target="tpu_custom_call" | custom-call | tf_op jit(solution)/shard_map/results/pallas_call | solution.py:705

commit v4 on v3

--- a/solution.py
+++ b/solution.py
@@ -22,24 +22,21 @@
 LAST = (((1,), (1,)), ((), ()))
 FIRST = (((0,), (0,)), ((), ()))
 
-ACT_WAY = (2, 2, 2)
 DPRE_WAY = (4, 2, 2)
 SPLIT_DACT = (0, 1)
 SPLIT_PRE = (0,)
-SPLIT_IN = (0, 2)
-SPLIT_OUT = (2,)
+SPLIT_IN = (2,)
 SPLIT_ACT = (0,)
 
 ORDER = (
-    "cotz", "cotc", "st1", "dact0a", "dact1a", "st3", "rsd0a", "coth", "rsd1a", "cotf", "pre0a",
-    "norh", "dact1b", "dact0b", "rsp0a", "norf", "rsd0b", "pre0b", "act0a", "rsp0b", "dgr0a",
-    "cph", "af0a", "act0b", "pre2", "za0", "nph", "af0b", "dgr0b", "df0a", "zaq0", "zd0", "ap0",
-    "pre1", "rsp2", "cpf", "zdn0", "df0b", "go0", "npf", "rsp1", "ngt1", "gso0", "act2", "zdq0",
-    "ngt0", "za2", "act1", "af2", "gi0", "af1", "gsi0a", "ap2", "geo0", "za1", "dact2", "zaq2",
-    "zaq1", "gsi0b", "rsd1b", "ap1", "gei0a", "rsd2", "go2", "dgr1", "go1", "gso2b", "zd1",
-    "gso2a", "dgr2", "out", "df1", "zd2", "gso1", "df2", "gei0b", "zdq1", "dp1", "dna", "zdq2",
-    "dp2", "dnb", "gi1", "dn2", "geo2b", "gi2", "gsi2a", "geo1", "fin", "gsi1", "gb", "gc",
-    "gei2a", "lo2", "gd", "geo2a", "gsi2b", "gei1", "ge", "t3", "lo3", "gei2b", "gz",
+    "cotc", "cotz", "st1", "dact0a", "dact1a", "rsd0a", "st3", "rsd1a", "cotf", "cyb", "pre0a",
+    "dact0b", "dact1b", "norh", "cya", "rsp0a", "rsd0b", "norf", "rsd1b", "pre0b", "act0a", "pre1",
+    "ngt0", "rsp0b", "af0a", "nph", "dgr0a", "act0b", "cybf", "dgr0b", "zd0", "rsp1", "cyaf",
+    "pre2", "zdn0", "df0a", "af0b", "df0b", "npf", "ngt1", "act1", "ya0", "zdq0", "dgr1", "zd1",
+    "cyc", "dact2", "af1", "gi0", "df1", "rsp2", "go0", "ya1", "zdq1", "rsd2", "gsi0", "act2",
+    "dgr2", "zd2", "geo0", "go1", "af2", "dna", "df2", "ya2", "dp1", "zdq2", "dp2", "dnb", "dn2",
+    "gi1", "gei0", "gi2", "go2", "gsi1", "fin", "gb", "gsi2b", "out", "gc", "lo2", "gd", "gsi2a",
+    "ge", "geo2", "gei1", "gei2b", "t3", "lo3", "geo1", "gei2a", "gz",
 )
 
 
@@ -50,8 +47,8 @@
 def kernel(
     tok, gain, win_hbm, wout_hbm, cot,
     layer_out, token_grad, gain_grad, gin_out, gout_out,
-    win, wout, nf, ngp, ngt, cg, ab, ag, dg, px, rx1, rx2, po, ro1, ro2, acc, slope,
-    pgi, pgo, gi1, gi2, go1, go2, stat, tails, gains, wsem_in, wsem_out, osem, ssem, rsem,
+    win, wout, nf, ngp, ngt, cg, ab, aq, dg, px, rx1, rx2, po, ro1, ro2, acc, slope,
+    pgi, pgo, gi1, gi2, go2, stat, tails, gains, wsem_in, wsem_out, osem, ssem, rsem,
 ):
     d, r, c = lax.axis_index("dp"), lax.axis_index("row"), lax.axis_index("col")
     zh, y = lax.div(d, 4), lax.rem(d, 4)
@@ -60,7 +57,7 @@
     yr, yl = lax.rem(y + 1, 4), lax.rem(y + 3, 4)
     cq, yq = lax.rem(c + 2, 4), lax.rem(y + 2, 4)
     XR, XL, XQ = (d, r, cr), (d, r, cl), (d, r, cq)
-    YR, YL = (zh * 4 + yr, r, c), (zh * 4 + yl, r, c)
+    YR, YL, YQ = (zh * 4 + yr, r, c), (zh * 4 + yl, r, c), (zh * 4 + yq, r, c)
     ZL, ZH = (d, (1 - zl) * 2 + co, c), ((1 - zh) * 4 + y, r, c)
     CO = (d, zl * 2 + 1 - co, c)
     YA = (zh * 4 + y + 1 - 2 * lax.rem(y, 2), r, c)
@@ -93,17 +90,20 @@
         gone = [id(cp) for cp in cps]
         sends[:] = [cp for cp in sends if id(cp) not in gone]
 
+    def place(k):
+        return 2 * lax.rem(k, 4) + lax.div(k, 4)
+
     def win_copy(j, k):
         return pltpu.make_async_copy(
             win_hbm.at[:, rows(k * 384 + j * 128, 128, 128)],
-            win.at[j, :, rows(k * 128, 128, 128)],
+            win.at[j, :, rows(place(k) * 128, 128, 128)],
             wsem_in.at[j, k],
         )
 
     def wout_copy(j, k):
         return pltpu.make_async_copy(
             wout_hbm.at[rows(k * 384 + j * 128, 128, 128)],
-            wout.at[j, rows(k * 128, 128, 128)],
+            wout.at[j, rows(place(k) * 128, 128, 128)],
             wsem_out.at[j, k],
         )
 
@@ -125,10 +125,10 @@
                 copy(j, k).wait()
 
     barrier = pltpu.get_barrier_semaphore()
-    for dev in (XR, XL, XQ, YR, YL, ZL, ZH, CO):
+    for dev in (XR, XL, XQ, YR, YL, YQ, ZL, ZH, CO):
         pl.semaphore_signal(barrier, inc=1, device_id=dev, device_id_type=MESH)
 
-    cg[0:2, 0] = cot[...].reshape(2, HALF, W)
+    cg[0, 0:2, 0] = cot[...].reshape(2, HALF, W)
     x = tok[...].astype(F32)
     lane = lax.broadcasted_iota(jnp.int32, (T, 128), 1)
 
@@ -136,7 +136,7 @@
         return jnp.where(lane == 0, a, jnp.where(lane == 1, b, 0.0))
 
     stat[0] = two(jnp.sum(x, axis=1, keepdims=True), jnp.sum(x * x, axis=1, keepdims=True))
-    pl.semaphore_wait(barrier, 8)
+    pl.semaphore_wait(barrier, 9)
 
     def mean_inverse():
         mean = stat[4, :, 0:1] / MODEL_WIDTH
@@ -167,13 +167,13 @@
         once(key + "1", V[key][2])
 
     def cotc():
-        V["cot"][0] = rc(slot(cg, 0), slot(cg, 1), CO)
+        V["cot"][0] = rc(slot(cg.at[0], 0), slot(cg.at[0], 1), CO)
 
     def cotz():
-        V["cot"][1] = rc(slot(cg, 0), slot(cg, 2), ZL)
+        V["cot"][1] = rc(slot(cg.at[0], 0), slot(cg.at[0], 2), ZL)
 
     S["cotc"], S["cotz"] = cotc, cotz
-    S["cotf"] = lambda: spread_on("cot", cg)
+    S["cotf"] = lambda: spread_on("cot", cg.at[0])
 
     def to_column(key, ref):
         V[key] = [rc(ref.at[0], ref.at[1 + i], dev) for i, dev in enumerate((XR, XL, XQ))]
@@ -195,18 +195,11 @@
     S["st1"], S["st3"] = st1, st3
     S["norf"] = lambda: spread_on("nor", nf)
 
-    def coth():
-        V["coth"] = rc(slot(cg, 0), slot(cg, 0, 4), ZH)
-
     def norh():
         V["norh"] = rc(
             nf.at[0:2, 0, :, rows((1 - zh) * FG, FG, 128)], slot(ngp, 0), ZH
         )
 
-    def cph():
-        recv(V["coth"])
-        spread("cp", cg, 4)
-
     def nph():
         recv(V["norh"])
         spread("np", ngp)
@@ -219,9 +212,28 @@
         whole("np")
         ngt[:, G:] = jnp.transpose(ngp[...].reshape(G, FG))
 
-    S["coth"], S["norh"], S["cph"], S["nph"] = coth, norh, cph, nph
+    S["norh"], S["nph"] = norh, nph
     S["ngt0"], S["ngt1"] = ngt0, ngt1
-    S["cpf"] = lambda: spread_on("cp", cg, 4)
+
+    def round_y(key, half):
+        own = cg.at[0, 0:2, half]
+        V[key] = [rc(own, cg.at[3, 0:2, half], YR), rc(own, cg.at[1, 0:2, half], YL)]
+
+    def round_y_on(key, half):
+        recv(V[key][0])
+        V[key].append(rc(cg.at[3, 0, half], cg.at[2, 0, half], YR))
+        recv(V[key][1])
+        V[key].append(rc(cg.at[1, 1, half], cg.at[2, 1, half], YL))
+
+    def cyc():
+        recv(*V["cya"][2:], *V["cyb"][2:])
+        V["cyc"] = rc(cg.at[1:4, 0:2], cg.at[1:4, 2:4], CO)
+
+    S["cya"] = lambda: round_y("cya", 0)
+    S["cyaf"] = lambda: round_y_on("cya", 0)
+    S["cyb"] = lambda: round_y("cyb", 1)
+    S["cybf"] = lambda: round_y_on("cyb", 1)
+    S["cyc"] = cyc
     S["npf"] = lambda: spread_on("np", ngp)
 
     def add(part, buf):
@@ -235,16 +247,16 @@
         own_chip(key) if h == 0 else whole(key)
         if j >= 2 and h != 1:
             drain(V["x1", kind, j - 2] + V["x2", kind, j - 2])
-        src = cg if kind == 0 else nf
+        src = cg.at[0] if kind == 0 else nf
         part = px.at[kind, j % 2]
 
         @pl.loop(0, H // 256)
         def _(n):
             at = rows(n * 256, 256, 256)
             if h is None:
-                left = src[0:4].reshape(G, W)
+                left = src[...].reshape(G, W)
             else:
-                left = src[0:4, h].reshape(G // 2, W)
+                left = src[:, h].reshape(G // 2, W)
             if kind == 0:
                 out = lax.dot_general(left, wout[j, at], LAST, preferred_element_type=F32)
             else:
@@ -356,55 +368,47 @@
         for h, _ in halves(j):
             ends((kind, j, h))
 
-    def over_z(kind, j, piece):
-        if kind == "a":
-            return rc(
-                ab.at[j, rows(piece * T, T), rows((1 - zh) * 512, 512, 128)],
-                ag.at[j, rows(G + piece * T, T)],
-                ZH,
-            )
+    def over_z(j, piece):
         return rc(dg.at[j, rows(piece * T, T)], dg.at[j, rows(G + piece * T, T)], ZH)
 
-    def partner_steps(kind, j, way):
-        ref = ag if kind == "a" else dg
-        key = (kind + "p", j)
-        name = "z%s%s%d"
+    def partner_steps(j, way):
+        key = ("dp", j)
 
         def z_own():
-            V["z", kind, j] = over_z(kind, j, c)
-
-        S["z%s%d" % (kind, j)] = z_own
+            V["z", j] = over_z(j, c)
+
+        S["zd%d" % j] = z_own
 
         def over_x():
-            once(("z", kind, j), V["z", kind, j])
-            both_ways(key, ref.at[j], G)
+            once(("z", j), V["z", j])
+            both_ways(key, dg.at[j], G)
 
         def opposite():
-            all_ends(kind, j)
-            V["zq", kind, j] = over_z(kind, j, cq)
+            all_ends("d", j)
+            V["zq", j] = over_z(j, cq)
 
         def neighbours():
             for h, _ in halves(j):
                 for i in (0, 1):
-                    once(((kind, j, h), i), V[kind, j, h][i])
-            V["zn", kind, j] = [over_z(kind, j, cl), over_z(kind, j, cr)]
+                    once((("d", j, h), i), V["d", j, h][i])
+            V["zn", j] = [over_z(j, cl), over_z(j, cr)]
 
         if way < 4:
-            S["%sp%d" % (kind, j)] = over_x
+            S["dp%d" % j] = over_x
         if way == 1:
-            S["%spf%d" % (kind, j)] = lambda: forward(key, ref.at[j], G)
+            S["dpf%d" % j] = lambda: forward(key, dg.at[j], G)
         if way > 1:
-            S[name % (kind, "q", j)] = opposite
+            S["zdq%d" % j] = opposite
         if way == 4:
-            S[name % (kind, "n", j)] = neighbours
+            S["zdn%d" % j] = neighbours
 
         def wait():
             if way == 1:
                 ends(key)
             elif way == 2:
-                recv(*V[key], V["zq", kind, j])
+                recv(*V[key], V["zq", j])
             else:
-                recv(V["z", kind, j], *V["zn", kind, j], V["zq", kind, j])
+                recv(V["z", j], *V["zn", j], V["zq", j])
 
         return wait
 
@@ -413,41 +417,61 @@
     def out_copy(key, j, k):
         if key == "o":
             return pltpu.make_async_copy(
-                go2.at[j, 0], gout_out.at[0, pl.ds(j * 128, 128)], osem.at[0, j, 0]
+                pgo.at[j, 1], gout_out.at[0, pl.ds(j * 128, 128)], osem.at[0, j, 0]
             )
         return pltpu.make_async_copy(
-            gi2.at[j, 0, :, pl.ds(k * 128, 128)],
+            gi2.at[j, 0, :, pl.ds((2 * (k % 4) + k // 4) * 128, 128)],
             gin_out.at[0, :, pl.ds(k * 384 + j * 128, 128)],
             osem.at[1, j, k],
         )
 
+    def grad_out_steps(j):
+        def spread_act():
+            all_ends("a", j)
+            V["ya", j] = [
+                rc(ab.at[j, :, rows(to * 256, 256, 256)], aq.at[j, i], dev)
+                for to, i, dev in ((yr, 3, YR), (yl, 1, YL), (yq, 2, YQ))
+            ]
+
+        def block(z):
+            at = rows(z * 128, 128, 128)
+            return lax.dot_general(
+                aq[j, :, :, at].reshape(4 * G, 128),
+                cg[...].reshape(4 * G, W),
+                FIRST,
+                preferred_element_type=F32,
+            ).astype(BF16)
+
+        def compute():
+            all_ends("a", j)
+            aq[j, 0] = ab[j, :, rows(y * 256, 256, 256)]
+            recv(*V["ya", j])
+            once("cyc", V["cyc"])
+            pgo[j, 0] = block(1 - zh)
+            V["o", j] = rc(pgo.at[j, 0], go2.at[j], ZH)
+            pgo[j, 1] = block(zh)
+
+        def end():
+            recv(V["o", j])
+            add(pgo.at[j, 1], go2.at[j])
+            cp = out_copy("o", j, 0)
+            cp.start()
+            ocps.append(cp)
+
+        S["ya%d" % j], S["go%d" % j], S["geo%d" % j] = spread_act, compute, end
+
     def gradient_steps(key, j, wait, split):
-        part, b1, b2, size = (
-            (pgo.at[j % 2], go1.at[j], go2.at[j], 128)
-            if key == "o"
-            else (pgi.at[j % 2], gi1.at[j], gi2.at[j], FB)
-        )
+        part, b1, b2, size = pgi.at[j % 2], gi1.at[j], gi2.at[j], FB
         pieces = (("a", 0), ("b", 1)) if split else (("", 0),)
         ps = size // len(pieces)
         h = ps // 2
 
         def block(b):
-            if key == "o":
-                at = rows(b * size, size, 128)
-                part[at] = lax.dot_general(
-                    ag[j, :, at], cg[...].reshape(2 * G, W), FIRST, preferred_element_type=F32
-                ).astype(BF16)
-            else:
-                at = rows(b * size, size)
-                part[at] = jnp.dot(ngt[at], dg[j], preferred_element_type=F32).astype(BF16)
+            at = rows(b * size, size)
+            part[at] = jnp.dot(ngt[at], dg[j], preferred_element_type=F32).astype(BF16)
 
         def compute():
-            if key == "o":
-                all_ends("a", j)
-                ag[j, 0:G] = ab[j, :, rows(zh * 512, 512, 128)]
-                whole("cp")
-            else:
-                all_ends("d", j)
+            all_ends("d", j)
             wait()
             if j >= 2:
                 drain(V["y", key, j - 2])
@@ -489,7 +513,7 @@
                 ).astype(BF16)
                 V["left", key, j] = V.get(("left", key, j), len(pieces)) - 1
                 if V["left", key, j] == 0:
-                    for k in range(1 if key == "o" else 8):
+                    for k in range(8):
                         cp = out_copy(key, j, k)
                         cp.start()
                         ocps.append(cp)
@@ -513,10 +537,8 @@
             S["dgr%d%s" % (j, tail)] = lambda h=h: dgelu(j, h)
             S["af%d%s" % (j, tail)] = lambda h=h: forward(("a", j, h), ab.at[j], 0, h)
             S["df%d%s" % (j, tail)] = lambda h=h: forward(("d", j, h), dg.at[j], 0, h)
-        wait_a = partner_steps("a", j, ACT_WAY[j])
-        wait_d = partner_steps("d", j, DPRE_WAY[j])
-        gradient_steps("o", j, wait_a, j in SPLIT_OUT)
-        gradient_steps("i", j, wait_d, j in SPLIT_IN)
+        grad_out_steps(j)
+        gradient_steps("i", j, partner_steps(j, DPRE_WAY[j]), j in SPLIT_IN)
 
     for j in range(NC):
         chunk_steps(j)
@@ -666,9 +688,9 @@
             pltpu.VMEM((4, 2, HALF, W), BF16),
             pltpu.VMEM((4, 2, HALF, FG), BF16),
             pltpu.VMEM((FG, 2 * G), BF16),
-            pltpu.VMEM((8, 2, HALF, W), BF16),
+            pltpu.VMEM((4, 4, 2, HALF, W), BF16),
             pltpu.VMEM((NC, G, H), BF16),
-            pltpu.VMEM((NC, 2 * G, 512), BF16),
+            pltpu.VMEM((NC, 4, G, 256), BF16),
             pltpu.VMEM((NC, 2 * G, H), BF16),
             pltpu.VMEM((2, 2, 4, 2, HALF, H), BF16),
             pltpu.VMEM((2, NC, 2, HALF, H), BF16),
@@ -679,11 +701,10 @@
             pltpu.VMEM((G, W), F32),
             pltpu.VMEM((2, T, H), F32),
             pltpu.VMEM((2, FG, H), BF16),
-            pltpu.VMEM((2, 512, W), BF16),
+            pltpu.VMEM((NC, 2, 128, W), BF16),
             pltpu.VMEM((NC, FB, H), BF16),
             pltpu.VMEM((NC, 2, FB, H), BF16),
             pltpu.VMEM((NC, 128, W), BF16),
-            pltpu.VMEM((NC, 2, 128, W), BF16),
             pltpu.VMEM((5, T, 128), F32),
             pltpu.VMEM((5, T, 128), F32),
             pltpu.VMEM((10, 8, W), F32),

time: 142 us -> 136 us (0.958)
  Pallas kernels: 141 us -> 135 us
    pallas_call x1, Pallas kernels: 138 us -> 132 us  [body(): pl.pallas_call(kernel, out_shape=(jax.ShapeDtypeStruct((T, W), BF16), jax...]
where the time goes in v4:
time: 136 us
  Pallas kernels  135 us (99%)
    pallas_call x1, Pallas kernels, body(): pl.pallas_call(kernel, out_shape=(jax.ShapeDtypeStruct((T, W), BF16), jax...  132 us
    pallas_call x1, Pallas kernels, body(): pl.pallas_call(copy_kernel, out_shape=tuple((jax.ShapeDtypeStruct(a.shape...  2.97 us

profile of v4, /device:TPU:1, one launch (start us, length us, event | category | flops | bytes accessed | tf_op | source)
XLA Modules:
  0.0 135.9 jit_solution(10125388133722875571)
XLA Ops:
  0.6 132.2 %feed_forward.1 = (bf16[96,1536]{1,0:T(8,128)(2,1)}, bf16[96,1536]{1,0:T(8,128)(2,1)}, f32[1536]{0:T(1024)}, bf16[1,192,3072]{2,1,0:T(8,128)(2,1)}, bf16[1,384,1536]{2,1,0:T(8,128)(2,1)}) custom-call(bf16[96,1536]{1,0:T(8,128)(2,1)} %tok.1, f32[1536]{0:T(1024)} %gain.1, bf16[1536,3072]{1,0:T(8,128)(2,1)} %win_hbm.1, bf16[3072,1536]{1,0:T(8,128)(2,1)} %wout_hbm.1, ...), custom_call_target="tpu_custom_call" | custom-call | flops 22000001024 | bytes 24000000 | tf_op jit(solution)/shard_map/feed_forward/pallas_call | solution.py:674
  132.8 3.0 %results.1 = (bf16[96,1536]{1,0:T(8,128)(2,1)}, bf16[96,1536]{1,0:T(8,128)(2,1)}, f32[1536]{0:T(1024)}, bf16[1,192,3072]{2,1,0:T(8,128)(2,1)}, bf16[1,384,1536]{2,1,0:T(8,128)(2,1)}) custom-call(bf16[96,1536]{1,0:T(8,128)(2,1)} %get-tuple-element.10.refs_0_, bf16[96,1536]{1,0:T(8,128)(2,1)} %get-tuple-element.11.refs_1_, f32[1536]{0:T(1024)} %get-tuple-element.12.refs_2_, ...), custom_call_target="tpu_custom_call" | custom-call | tf_op jit(solution)/shard_map/results/pallas_call | solution.py:726

commit v5 on v4

--- a/solution.py
+++ b/solution.py
@@ -22,21 +22,21 @@
 LAST = (((1,), (1,)), ((), ()))
 FIRST = (((0,), (0,)), ((), ()))
 
-DPRE_WAY = (4, 2, 2)
+DPRE_WAY = (4, 4, 2)
 SPLIT_DACT = (0, 1)
 SPLIT_PRE = (0,)
 SPLIT_IN = (2,)
 SPLIT_ACT = (0,)
 
 ORDER = (
-    "cotc", "cotz", "st1", "dact0a", "dact1a", "rsd0a", "st3", "rsd1a", "cotf", "cyb", "pre0a",
-    "dact0b", "dact1b", "norh", "cya", "rsp0a", "rsd0b", "norf", "rsd1b", "pre0b", "act0a", "pre1",
-    "ngt0", "rsp0b", "af0a", "nph", "dgr0a", "act0b", "cybf", "dgr0b", "zd0", "rsp1", "cyaf",
-    "pre2", "zdn0", "df0a", "af0b", "df0b", "npf", "ngt1", "act1", "ya0", "zdq0", "dgr1", "zd1",
-    "cyc", "dact2", "af1", "gi0", "df1", "rsp2", "go0", "ya1", "zdq1", "rsd2", "gsi0", "act2",
-    "dgr2", "zd2", "geo0", "go1", "af2", "dna", "df2", "ya2", "dp1", "zdq2", "dp2", "dnb", "dn2",
-    "gi1", "gei0", "gi2", "go2", "gsi1", "fin", "gb", "gsi2b", "out", "gc", "lo2", "gd", "gsi2a",
-    "ge", "geo2", "gei1", "gei2b", "t3", "lo3", "geo1", "gei2a", "gz",
+    "cotc", "cotz", "st1", "cya", "dact0a", "dact1a", "st3", "rsd0a", "pre0a", "cotf", "rsd1a",
+    "dact0b", "rsp0a", "dact1b", "norh", "cyaf", "cyb", "norf", "rsd0b", "pre0b", "act0a", "rsp0b",
+    "af0a", "nph", "dgr0a", "act0b", "dgr0b", "zd0", "cybf", "pre1", "af0b", "zdn0", "npf", "df0b",
+    "df0a", "cyc", "rsp1", "rsd1b", "ya0", "ngt0", "zdq0", "pre2", "ngt1", "act1", "dgr1", "zd1",
+    "dact2", "go0", "af1", "gi0", "zdn1", "df1", "rsp2", "ya1", "zdq1", "rsd2", "dna", "gsi0",
+    "act2", "dgr2", "zd2", "go1", "gi1", "af2", "df2", "dp2", "ya2", "zdq2", "dnb", "dn2", "gei0",
+    "gsi1", "gi2", "go2", "out", "fin", "gsi2a", "gb", "lo2", "gsi2b", "t3", "gei1", "geo0",
+    "gei2a", "gc", "geo1", "gei2b", "geo2", "gz", "lo3",
 )
 
 
@@ -48,7 +48,7 @@
     tok, gain, win_hbm, wout_hbm, cot,
     layer_out, token_grad, gain_grad, gin_out, gout_out,
     win, wout, nf, ngp, ngt, cg, ab, aq, dg, px, rx1, rx2, po, ro1, ro2, acc, slope,
-    pgi, pgo, gi1, gi2, go2, stat, tails, gains, wsem_in, wsem_out, osem, ssem, rsem,
+    pgi, pgo, gi1, gi2, go2, stat, tails, sums, gains, result, wsem_in, wsem_out, osem, rsem_out, ssem, rsem,
 ):
     d, r, c = lax.axis_index("dp"), lax.axis_index("row"), lax.axis_index("col")
     zh, y = lax.div(d, 4), lax.rem(d, 4)
@@ -59,9 +59,7 @@
     XR, XL, XQ = (d, r, cr), (d, r, cl), (d, r, cq)
     YR, YL, YQ = (zh * 4 + yr, r, c), (zh * 4 + yl, r, c), (zh * 4 + yq, r, c)
     ZL, ZH = (d, (1 - zl) * 2 + co, c), ((1 - zh) * 4 + y, r, c)
-    CO = (d, zl * 2 + 1 - co, c)
-    YA = (zh * 4 + y + 1 - 2 * lax.rem(y, 2), r, c)
-    YB = (zh * 4 + 3 - y, r, c)
+    CO, ZLO = (d, zl * 2 + 1 - co, c), (d, (1 - zl) * 2 + 1 - co, c)
 
     def slot(ref, i, first=0):
         return ref.at[pl.ds(first + 2 * (i % 2), 2), i // 2]
@@ -85,10 +83,15 @@
             cp.wait_recv()
 
     def drain(cps):
-        for cp in cps:
-            cp.wait_send()
         gone = [id(cp) for cp in cps]
+        for cp in sends:
+            if id(cp) in gone:
+                cp.wait_send()
         sends[:] = [cp for cp in sends if id(cp) not in gone]
+
+    barrier = pltpu.get_barrier_semaphore()
+    for dev in (XR, XL, XQ, YR, YL, YQ, ZL, ZLO, ZH, CO):
+        pl.semaphore_signal(barrier, inc=1, device_id=dev, device_id_type=MESH)
 
     def place(k):
         return 2 * lax.rem(k, 4) + lax.div(k, 4)
@@ -107,8 +110,7 @@
             wsem_out.at[j, k],
         )
 
-    for j in range(NC):
-
+    def load(j):
         @pl.loop(0, 8)
         def _(k):
             wout_copy(j, k).start()
@@ -124,23 +126,26 @@
             def _(k):
                 copy(j, k).wait()
 
-    barrier = pltpu.get_barrier_semaphore()
-    for dev in (XR, XL, XQ, YR, YL, YQ, ZL, ZH, CO):
-        pl.semaphore_signal(barrier, inc=1, device_id=dev, device_id_type=MESH)
-
     cg[0, 0:2, 0] = cot[...].reshape(2, HALF, W)
+    load(0)
     x = tok[...].astype(F32)
     lane = lax.broadcasted_iota(jnp.int32, (T, 128), 1)
 
-    def two(a, b):
-        return jnp.where(lane == 0, a, jnp.where(lane == 1, b, 0.0))
-
-    stat[0] = two(jnp.sum(x, axis=1, keepdims=True), jnp.sum(x * x, axis=1, keepdims=True))
-    pl.semaphore_wait(barrier, 9)
+    def two_rows(a, b):
+        both = jnp.where(lane == 0, a, jnp.where(lane == 1, b, 0.0))
+        both = jnp.concatenate([both, jnp.zeros((128 - T, 128), F32)], axis=0)
+        return jnp.transpose(both)[0:8]
+
+    def two_columns(both):
+        both = jnp.concatenate([both, jnp.zeros((120, 128), F32)], axis=0)
+        return jnp.transpose(both)[0:T]
+
+    stat[0] = two_rows(jnp.sum(x, axis=1, keepdims=True), jnp.sum(x * x, axis=1, keepdims=True))
+    pl.semaphore_wait(barrier, 10)
 
     def mean_inverse():
-        mean = stat[4, :, 0:1] / MODEL_WIDTH
-        return mean, lax.rsqrt(stat[4, :, 1:2] / MODEL_WIDTH - mean * mean + EPS)
+        mean = sums[0, :, 0:1] / MODEL_WIDTH
+        return mean, lax.rsqrt(sums[0, :, 1:2] / MODEL_WIDTH - mean * mean + EPS)
 
     S = {}
 
@@ -178,15 +183,17 @@
     def to_column(key, ref):
         V[key] = [rc(ref.at[0], ref.at[1 + i], dev) for i, dev in enumerate((XR, XL, XQ))]
 
-    def of_column(key, ref):
+    def of_column(key, ref, i):
         recv(*V[key])
-        ref[4] = (ref[0] + ref[3]) + (ref[1] + ref[2])
+        sums[i] = two_columns((ref[0] + ref[3]) + (ref[1] + ref[2]))
 
     def st1():
         to_column("sa", stat)
+        for j in range(1, NC):
+            load(j)
 
     def st3():
-        of_column("sa", stat)
+        of_column("sa", stat, 0)
         mean, inverse = mean_inverse()
         normed = ((tok[...].astype(F32) - mean) * inverse * gain[...].reshape(1, W)).astype(BF16)
         nf[0:2, 0] = normed.reshape(2, HALF, W)
@@ -598,53 +605,61 @@
     def dn2():
         V["dn2"] = row_second(1, "dn1")
 
+    def leave(i, out):
+        cp = pltpu.make_async_copy(result.at[i], out, rsem_out.at[i])
+        cp.start()
+        ocps.append(cp)
+
     def lo3():
         recv(V["lo2"])
-        layer_out[...] = (tok[...].astype(F32) + row_sum(0)).astype(BF16)
+        result[0] = (tok[...].astype(F32) + row_sum(0)).astype(BF16)
+        leave(0, layer_out)
 
     def fin():
         recv(V["dn2"])
         mean, inverse = mean_inverse()
         dnorm = row_sum(1)
         xhat = (tok[...].astype(F32) - mean) * inverse
-        gains[0] = jnp.sum((dnorm * xhat).reshape(T // 8, 8, W), axis=0)
-        V["ga"] = rc(gains.at[0], gains.at[1], CO)
+        gains[r] = jnp.sum(dnorm * xhat, axis=0, keepdims=True)
+        V["ga"] = [rc(gains.at[r], gains.at[r], dev) for dev in (CO, ZL, ZLO)]
         dxhat = dnorm * gain[...].reshape(1, W)
-        tails[0] = two(
+        tails[0] = two_rows(
             jnp.sum(dxhat, axis=1, keepdims=True), jnp.sum(dxhat * xhat, axis=1, keepdims=True)
         )
         to_column("ta", tails)
 
     def t3():
-        of_column("ta", tails)
+        of_column("ta", tails, 1)
         mean, inverse = mean_inverse()
-        first = tails[4, :, 0:1] / MODEL_WIDTH
-        second = tails[4, :, 1:2] / MODEL_WIDTH
+        first = sums[1, :, 0:1] / MODEL_WIDTH
+        second = sums[1, :, 1:2] / MODEL_WIDTH
         xhat = (tok[...].astype(F32) - mean) * inverse
-        token_grad[...] = (
+        result[1] = (
             cot[...].astype(F32) + inverse * (row_sum(1) * gain[...].reshape(1, W) - first - xhat * second)
         ).astype(BF16)
-
-    def gain_step(i, old, new, dev):
-        def step():
-            recv(V[old])
-            gains[2 * i + 2] = gains[2 * i] + gains[2 * i + 1]
-            V[new] = rc(gains.at[2 * i + 2], gains.at[2 * i + 3], dev)
-
-        return step
+        leave(1, token_grad)
+
+    def gb():
+        recv(*V["ga"])
+        gains[4 + zh] = (gains[0] + gains[1]) + (gains[2] + gains[3])
+        V["gb"] = rc(gains.at[4 + zh], gains.at[4 + zh], ZH)
+
+    def gc():
+        recv(V["gb"])
+        gains[6 + y] = gains[4] + gains[5]
+        V["gc"] = [rc(gains.at[6 + y], gains.at[6 + y], dev) for dev in (YR, YL, YQ)]
 
     def gz():
-        recv(V["ge"])
-        gain_grad[...] = jnp.sum(gains[8] + gains[9], axis=0)
+        recv(*V["gc"])
+        gain_grad[...] = jnp.sum((gains[6] + gains[7]) + (gains[8] + gains[9]), axis=0)
 
     S.update(out=out, dna=dna, dnb=dnb, lo2=lo2, dn2=dn2, lo3=lo3, fin=fin, t3=t3, gz=gz)
-    S["gb"] = gain_step(0, "ga", "gb", ZL)
-    S["gc"] = gain_step(1, "gb", "gc", ZH)
-    S["gd"] = gain_step(2, "gc", "gd", YA)
-    S["ge"] = gain_step(3, "gd", "ge", YB)
+    S["gb"], S["gc"] = gb, gc
 
     assert sorted(S) == sorted(ORDER)
-    for name in ORDER:
+    for i, name in enumerate(ORDER):
+        if i >= len(ORDER) - 12:
+            drain(sends[:-16])
         S[name]()
     drain(list(sends))
     for cp in ocps:
@@ -681,7 +696,7 @@
             jax.ShapeDtypeStruct((1, NC * 128, W), BF16),
         ),
         in_specs=[vm, vm, hbm, hbm, vm],
-        out_specs=(vm, vm, vm, hbm, hbm),
+        out_specs=(hbm, hbm, vm, hbm, hbm),
         scratch_shapes=[
             pltpu.VMEM((NC, W, H), BF16),
             pltpu.VMEM((NC, H, W), BF16),
@@ -705,12 +720,15 @@
             pltpu.VMEM((NC, FB, H), BF16),
             pltpu.VMEM((NC, 2, FB, H), BF16),
             pltpu.VMEM((NC, 128, W), BF16),
-            pltpu.VMEM((5, T, 128), F32),
-            pltpu.VMEM((5, T, 128), F32),
-            pltpu.VMEM((10, 8, W), F32),
+            pltpu.VMEM((4, 8, 128), F32),
+            pltpu.VMEM((4, 8, 128), F32),
+            pltpu.VMEM((2, T, 128), F32),
+            pltpu.VMEM((10, 1, W), F32),
+            pltpu.VMEM((2, T, W), BF16),
             pltpu.SemaphoreType.DMA((NC, 8)),
             pltpu.SemaphoreType.DMA((NC, 8)),
             pltpu.SemaphoreType.DMA((2, NC, 8)),
+            pltpu.SemaphoreType.DMA((2,)),
             pltpu.SemaphoreType.DMA((N_COPIES,)),
             pltpu.SemaphoreType.DMA((N_COPIES,)),
         ],

time: 136 us -> 131 us (0.963)
  Pallas kernels: 135 us -> 130 us
    pallas_call x1, Pallas kernels: 132 us -> 127 us  [body(): pl.pallas_call(kernel, out_shape=(jax.ShapeDtypeStruct((T, W), BF16), jax...]
where the time goes in v5:
time: 131 us
  Pallas kernels  130 us (99%)
    pallas_call x1, Pallas kernels, body(): pl.pallas_call(kernel, out_shape=(jax.ShapeDtypeStruct((T, W), BF16), jax...  127 us
    pallas_call x1, Pallas kernels, body(): pl.pallas_call(copy_kernel, out_shape=tuple((jax.ShapeDtypeStruct(a.shape...  2.97 us

profile of v5, /device:TPU:1, one launch (start us, length us, event | category | flops | bytes accessed | tf_op | source)
XLA Modules:
  0.0 130.5 jit_solution(17884429972545177598)
XLA Ops:
  0.6 126.8 %feed_forward.1 = (bf16[96,1536]{1,0:T(8,128)(2,1)}, bf16[96,1536]{1,0:T(8,128)(2,1)}, f32[1536]{0:T(1024)}, bf16[1,192,3072]{2,1,0:T(8,128)(2,1)}, bf16[1,384,1536]{2,1,0:T(8,128)(2,1)}) custom-call(bf16[96,1536]{1,0:T(8,128)(2,1)} %tok.1, f32[1536]{0:T(1024)} %gain.1, bf16[1536,3072]{1,0:T(8,128)(2,1)} %win_hbm.1, bf16[3072,1536]{1,0:T(8,128)(2,1)} %wout_hbm.1, ...), custom_call_target="tpu_custom_call" | custom-call | flops 22000001024 | bytes 24000000 | tf_op jit(solution)/shard_map/feed_forward/pallas_call | solution.py:689
  127.4 3.0 %results.1 = (bf16[96,1536]{1,0:T(8,128)(2,1)}, bf16[96,1536]{1,0:T(8,128)(2,1)}, f32[1536]{0:T(1024)}, bf16[1,192,3072]{2,1,0:T(8,128)(2,1)}, bf16[1,384,1536]{2,1,0:T(8,128)(2,1)}) custom-call(bf16[96,1536]{1,0:T(8,128)(2,1)} %get-tuple-element.10.refs_0_, bf16[96,1536]{1,0:T(8,128)(2,1)} %get-tuple-element.11.refs_1_, f32[1536]{0:T(1024)} %get-tuple-element.12.refs_2_, ...), custom_call_target="tpu_custom_call" | custom-call | tf_op jit(solution)/shard_map/results/pallas_call | solution.py:744

commit v6 on v5

--- a/solution.py
+++ b/solution.py
@@ -29,14 +29,14 @@
 SPLIT_ACT = (0,)
 
 ORDER = (
-    "cotc", "cotz", "st1", "cya", "dact0a", "dact1a", "st3", "rsd0a", "pre0a", "cotf", "rsd1a",
-    "dact0b", "rsp0a", "dact1b", "norh", "cyaf", "cyb", "norf", "rsd0b", "pre0b", "act0a", "rsp0b",
-    "af0a", "nph", "dgr0a", "act0b", "dgr0b", "zd0", "cybf", "pre1", "af0b", "zdn0", "npf", "df0b",
-    "df0a", "cyc", "rsp1", "rsd1b", "ya0", "ngt0", "zdq0", "pre2", "ngt1", "act1", "dgr1", "zd1",
-    "dact2", "go0", "af1", "gi0", "zdn1", "df1", "rsp2", "ya1", "zdq1", "rsd2", "dna", "gsi0",
-    "act2", "dgr2", "zd2", "go1", "gi1", "af2", "df2", "dp2", "ya2", "zdq2", "dnb", "dn2", "gei0",
-    "gsi1", "gi2", "go2", "out", "fin", "gsi2a", "gb", "lo2", "gsi2b", "t3", "gei1", "geo0",
-    "gei2a", "gc", "geo1", "gei2b", "geo2", "gz", "lo3",
+    "cotc", "cotz", "st1", "dact0a", "dact1a", "st3", "rsd0a", "norh", "cya", "pre0a", "cotf",
+    "rsd1a", "dact0b", "cyb", "dact1b", "rsp0a", "norf", "rsd0b", "pre0b", "act0a", "rsp0b", "nph",
+    "af0a", "cyaf", "dgr0a", "act0b", "dgr0b", "cybf", "ngt0", "zd0", "pre1", "af0b", "zdn0",
+    "df0b", "df0a", "npf", "rsp1", "rsd1b", "ya0", "zdq0", "ngt1", "pre2", "cyc", "act1", "dgr1",
+    "zd1", "go0", "af1", "gi0", "dact2", "df1", "ya1", "zdn1", "rsp2", "gsi0", "rsd2", "zdq1",
+    "act2", "dgr2", "zd2", "dna", "go1", "af2", "gi1", "df2", "ya2", "gsi1", "zdq2", "dnb", "gei0",
+    "geo1", "dn2", "geo0", "dp2", "out", "go2", "gi2", "fin", "t3", "gsi2a", "gsi2b", "gb", "lo2",
+    "geo2", "gei2a", "gc", "gei1", "gei2b", "gz", "lo3",
 )
 
 
@@ -257,9 +257,9 @@
         src = cg.at[0] if kind == 0 else nf
         part = px.at[kind, j % 2]
 
-        @pl.loop(0, H // 256)
+        @pl.loop(0, H // 1024)
         def _(n):
-            at = rows(n * 256, 256, 256)
+            at = rows(n * 1024, 1024, 1024)
             if h is None:
                 left = src[...].reshape(G, W)
             else:
@@ -269,9 +269,9 @@
             else:
                 out = jnp.dot(left, win[j, :, at], preferred_element_type=F32)
             if h is None:
-                part[:, :, :, at] = out.astype(BF16).reshape(4, 2, HALF, 256)
+                part[:, :, :, at] = out.astype(BF16).reshape(4, 2, HALF, 1024)
             else:
-                part[:, h, :, at] = out.astype(BF16).reshape(4, HALF, 256)
+                part[:, h, :, at] = out.astype(BF16).reshape(4, HALF, 1024)
 
         buf = rx1.at[kind, j]
         if h is None:
@@ -554,13 +554,13 @@
         for j in range(NC):
             all_ends("a", j)
 
-        @pl.loop(0, W // 256)
+        @pl.loop(0, W // 768)
         def _(n):
-            at = rows(n * 256, 256, 256)
+            at = rows(n * 768, 768, 768)
             total = jnp.dot(ab[0], wout[0, :, at], preferred_element_type=F32)
             for j in range(1, NC):
                 total += jnp.dot(ab[j], wout[j, :, at], preferred_element_type=F32)
-            po[0, :, :, :, at] = total.astype(BF16).reshape(4, 2, HALF, 256)
+            po[0, :, :, :, at] = total.astype(BF16).reshape(4, 2, HALF, 768)
 
         V["lo1"] = rc(po.at[0, 2:4], ro1.at[0], CO)
 
@@ -568,9 +568,9 @@
         for j in (0, 1):
             all_ends("d", j)
 
-        @pl.loop(0, W // 256)
+        @pl.loop(0, W // 768)
         def _(n):
-            at = rows(n * 256, 256, 256)
+            at = rows(n * 768, 768, 768)
             acc[:, at] = sum(
                 lax.dot_general(dg[j, 0:G], win[j, at], LAST, preferred_element_type=F32)
                 for j in (0, 1)
@@ -579,13 +579,13 @@
     def dnb():
         all_ends("d", 2)
 
-        @pl.loop(0, W // 256)
+        @pl.loop(0, W // 768)
         def _(n):
-            at = rows(n * 256, 256, 256)
+            at = rows(n * 768, 768, 768)
             total = acc[:, at] + lax.dot_general(
                 dg[2, 0:G], win[2, at], LAST, preferred_element_type=F32
             )
-            po[1, :, :, :, at] = total.astype(BF16).reshape(4, 2, HALF, 256)
+            po[1, :, :, :, at] = total.astype(BF16).reshape(4, 2, HALF, 768)
 
         V["dn1"] = rc(po.at[1, 2:4], ro1.at[1], CO)
 
@@ -670,10 +670,20 @@
 N_COPIES = 230
 
 
+def parts(i, ref):
+    if i < 3:
+        return [ref]
+    n = ref.shape[1] // 4
+    return [ref.at[0, pl.ds(k * n, n)] for k in range(4)]
+
+
 def copy_kernel(*refs):
     src, dst, via, (one, two) = refs[:5], refs[5:10], refs[10:15], refs[15:]
-    first = [pltpu.make_async_copy(src[i], via[i], one.at[i]) for i in range(5)]
-    then = [pltpu.make_async_copy(via[i], dst[i], two.at[i]) for i in range(5)]
+    moves = []
+    for i in (3, 4, 0, 1, 2):
+        moves += list(zip(parts(i, src[i]), parts(i, via[i]), parts(i, dst[i])))
+    first = [pltpu.make_async_copy(a, v, one.at[k]) for k, (a, v, _) in enumerate(moves)]
+    then = [pltpu.make_async_copy(v, b, two.at[k]) for k, (_, v, b) in enumerate(moves)]
     for cp in first:
         cp.start()
     for a, b in zip(first, then):
@@ -747,7 +757,7 @@
         in_specs=[hbm] * 5,
         out_specs=(hbm,) * 5,
         scratch_shapes=[pltpu.VMEM(a.shape, a.dtype) for a in arrays]
-        + [pltpu.SemaphoreType.DMA((5,)), pltpu.SemaphoreType.DMA((5,))],
+        + [pltpu.SemaphoreType.DMA((11,)), pltpu.SemaphoreType.DMA((11,))],
         name="results",
     )(*arrays)
 

time: 131 us -> 130 us (level)
  Pallas kernels: 130 us -> 127 us
    pallas_call x1, Pallas kernels: 127 us -> 125 us  [body(): pl.pallas_call(kernel, out_shape=(jax.ShapeDtypeStruct((T, W), BF16), jax...]
where the time goes in v6:
time: 130 us; the launch traced here: 128 us
  Pallas kernels  127 us (98%)
    pallas_call x1, Pallas kernels, body(): pl.pallas_call(kernel, out_shape=(jax.ShapeDtypeStruct((T, W), BF16), jax...  125 us
    pallas_call x1, Pallas kernels, body(): pl.pallas_call(copy_kernel, out_shape=tuple((jax.ShapeDtypeStruct(a.shape...  2.75 us

profile of v6, /device:TPU:1, one launch (start us, length us, event | category | flops | bytes accessed | tf_op | source)
XLA Modules:
  0.0 128.3 jit_solution(5807014160842245109)
XLA Ops:
  0.6 124.7 %feed_forward.1 = (bf16[96,1536]{1,0:T(8,128)(2,1)}, bf16[96,1536]{1,0:T(8,128)(2,1)}, f32[1536]{0:T(1024)}, bf16[1,192,3072]{2,1,0:T(8,128)(2,1)}, bf16[1,384,1536]{2,1,0:T(8,128)(2,1)}) custom-call(bf16[96,1536]{1,0:T(8,128)(2,1)} %tok.1, f32[1536]{0:T(1024)} %gain.1, bf16[1536,3072]{1,0:T(8,128)(2,1)} %win_hbm.1, bf16[3072,1536]{1,0:T(8,128)(2,1)} %wout_hbm.1, ...), custom_call_target="tpu_custom_call" | custom-call | flops 22000001024 | bytes 24000000 | tf_op jit(solution)/shard_map/feed_forward/pallas_call | solution.py:699
  125.4 2.7 %results.1 = (bf16[96,1536]{1,0:T(8,128)(2,1)}, bf16[96,1536]{1,0:T(8,128)(2,1)}, f32[1536]{0:T(1024)}, bf16[1,192,3072]{2,1,0:T(8,128)(2,1)}, bf16[1,384,1536]{2,1,0:T(8,128)(2,1)}) custom-call(bf16[96,1536]{1,0:T(8,128)(2,1)} %get-tuple-element.10.refs_0_, bf16[96,1536]{1,0:T(8,128)(2,1)} %get-tuple-element.11.refs_1_, f32[1536]{0:T(1024)} %get-tuple-element.12.refs_2_, ...), custom_call_target="tpu_custom_call" | custom-call | tf_op jit(solution)/shard_map/results/pallas_call | solution.py:754
